TPU v7x, 256 devices: a whole 4x4x8 slice. The times are simulated.
256 devices in a mesh: slab: 4 (over z_lo), tile: 64 (over y, z_hi, x, core).
Axes of the slice: x: 4, y: 4, z: 8 (z_hi: 2, z_lo: 4; z = z_hi * 4 + z_lo), core: 2. Of those that a mesh axis runs over, the one named last changes fastest.
Arguments:
- features: bfloat16 [2048, 64, 512], P(('slab', 'tile')), may hold values from -6 to 6
- cotangent: bfloat16 [2048, 64, 512], P(('slab', 'tile')), may hold values from -6 to 6
- weight: bfloat16 [64, 1728], replicated, may hold values from -0.15625 to 0.15625
- block_table: int32 [4, 128, 8], replicated, may hold values from -1 to 7, as said below
Outputs:
- conv_out: bfloat16 [2048, 64, 512], P(('slab', 'tile'))
- grad_features: bfloat16 [2048, 64, 512], P(('slab', 'tile'))
- grad_weight: float32 [64, 1728], replicated
Inputs may be any that keep to these rules, and one draw needn't show every extreme that they name: `block_table`: -1 marks an inactive block. An active block (bz, by, bx) holds (by modulo 2) * 4 plus the number of active blocks before it along x in its row (bz, by). Every row has at least one and at most 4 active blocks; all rows of one block layer bz share an active block in one column. Some row with by modulo 2 = 1 has exactly 4.
All inputs are finite; a program needn't handle non-finite values.
Results may differ from a plain program's by a relative error of at most 0.001.
Values may be sent and summed in bfloat16 or wider, within the bound.
No kernel may reach another device: no remote copies, remote signals or barrier semaphores. Data moves between devices by JAX's collectives and lax.ppermute only.
A program may use at most 64 MiB of HBM per device.

v0:
```python
import jax
import jax.numpy as jnp
import numpy as np
from jax import lax
from jax.experimental import pallas as pl
from jax.experimental.pallas import tpu as pltpu
from jax.sharding import PartitionSpec as P

LX = 8
YR = 2
BF = jnp.bfloat16
F32 = jnp.float32
AXES = ("slab", "tile")
N_DEV = 256
VMEM_LIMIT = 48 * 1024 * 1024
SHIFTS = [dy * 10 + dx for dy in (-1, 0, 1) for dx in (-1, 0, 1)]


def params():
    return pltpu.CompilerParams(vmem_limit_bytes=VMEM_LIMIT)


def iota(shape, dim):
    return lax.broadcasted_iota(jnp.int32, shape, dim)


def halves(a, b, right):
    cut = slice(64, 128) if right else slice(0, 64)
    return jnp.concatenate([a[:, cut], b[:, cut]], axis=1)


def faces_kernel(x0_ref, x3_ref, g0_ref, g3_ref, low_ref, high_ref):
    for s in range(8):
        low_ref[s] = halves(x0_ref[s], g0_ref[s], False)
        high_ref[s] = halves(x3_ref[s], g3_ref[s], True)


def faces(x, g):
    def at(t):
        return pl.BlockSpec((8, 64, 128), lambda i, t=t: (0, 0, t))

    whole = pl.BlockSpec((8, 64, 128), lambda i: (0, 0, 0))
    face = jax.ShapeDtypeStruct((8, 64, 128), BF)
    return pl.pallas_call(
        faces_kernel,
        grid=(1,),
        in_specs=[at(0), at(3), at(0), at(3)],
        out_specs=[whole, whole],
        out_shape=[face, face],
        compiler_params=params(),
        name="faces",
    )(x, x, g, g)


def edges_kernel(core_ref, x_ref, g_ref, below_ref, above_ref, pair_ref, other_ref):
    chunk = iota((1024, 128), 0) // 128
    lane = iota((1024, 128), 0) % 128
    to = iota((1024, 128), 1)

    def picks(y):
        here = (lane // 8) % 8 == y
        edge = (lane // 64) * 64 + chunk * 8 + lane % 8
        line = (chunk // 4) * 64 + (lane // 64) * 32 + (chunk % 4) * 8 + lane % 8
        return [
            jnp.where(here & (at == to), 1.0, 0.0).astype(BF) for at in (edge, line)
        ]

    found = []
    for first, y in ((4, 7), (0, 0)):
        edge, line = picks(y)
        rows = [
            jnp.concatenate(
                [ref[first + s, :, 128 * t : 128 * t + 128] for ref in (x_ref, g_ref) for s in range(4)],
                axis=1,
            )
            for t in range(4)
        ]
        lines = jnp.concatenate(
            [ref[first + s] for ref in (below_ref, above_ref) for s in range(4)], axis=1
        )
        main = jnp.dot(jnp.concatenate(rows, axis=0), edge, preferred_element_type=F32)
        last = jnp.dot(lines, line, preferred_element_type=F32)
        found.append(jnp.concatenate([main, last], axis=0))
    up, down = found
    odd = core_ref[0]
    pair_ref[...] = jnp.where(odd == 0, up, down).astype(BF)
    other_ref[...] = jnp.where(odd == 0, down, up).astype(BF)


def edges(core, x, g, below, above):
    out = jax.ShapeDtypeStruct((320, 128), BF)
    vmem = pl.BlockSpec(memory_space=pltpu.VMEM)
    return pl.pallas_call(
        edges_kernel,
        in_specs=[pl.BlockSpec(memory_space=pltpu.SMEM)] + [vmem] * 4,
        out_specs=[vmem, vmem],
        out_shape=[out, out],
        compiler_params=params(),
        name="edges",
    )(core, x, g, below, above)


def places_kernel(core_ref, table_ref, place_ref):
    odd = core_ref[0]
    lane = iota((8, 128), 1)
    ly = lane // 10 - 1
    lx = lane % 10 - 1
    used = lane < 100
    y_class = jnp.where(ly < 0, 0, jnp.where(ly > 7, 2, 1))
    x_class = jnp.where(lx < 0, 0, jnp.where(lx > 7, 2, 1))
    near = jnp.where(used, y_class * 3 + x_class, -1)
    inner_x = lx & 7
    inner = (ly & 7) * 8 + inner_x
    rows = iota((768, 128), 0)
    for s in range(8):
        r = s // 4
        column = jnp.int32(-10)
        for b in range(8):
            column = jnp.where(table_ref[(4 + r + 1) * 8 + b] == s, b, column)
        for d in range(3):
            source = jnp.full((8, 128), -1, jnp.int32)
            for dy in range(3):
                row = r + dy
                for dx in range(3):
                    at = column + (dx - 1)
                    inside = (at >= 0) & (at < LX)
                    held = table_ref[(d * 4 + row) * 8 + jnp.clip(at, 0, LX - 1)]
                    fine = inside & (held >= 0)
                    if row in (1, 2):
                        base = jnp.where(fine, held * 64, -10000)
                        value = base + inner
                    else:
                        side = 1 - odd if row == 0 else odd
                        base = jnp.where(fine, 512 + side * 128 + (held & 3) * 8, -10000)
                        value = base + inner_x
                    source = jnp.where(near == dy * 3 + dx, value, source)
            place_ref[d, :, 128 * s : 128 * s + 128] = jnp.where(
                rows == source[0:1], 1.0, 0.0
            ).astype(BF)


def places(core, window):
    smem = pl.BlockSpec(memory_space=pltpu.SMEM)
    return pl.pallas_call(
        places_kernel,
        in_specs=[smem, smem],
        out_specs=pl.BlockSpec(memory_space=pltpu.VMEM),
        out_shape=jax.ShapeDtypeStruct((3, 768, 1024), BF),
        compiler_params=params(),
        name="places",
    )(core, window)


def taps(planes_ref, slot, z_from, z_count):
    at = pl.ds(pl.multiple_of(slot * 128, 128), 128)
    return jnp.concatenate(
        [
            jnp.concatenate(
                [planes_ref[64 * (z + dz) : 64 * (z + dz) + 64, at] for z in range(z_from, z_from + z_count)],
                axis=1,
            )
            for dz in range(3)
        ],
        axis=0,
    )


def terms_kernel(scale_ref, place_ref, x_ref, g_ref, below_ref, above_ref, pair_ref, other_ref, planes_ref, terms_ref, left_ref, total_ref):
    def fill(row, tiles, right, band, lane_group):
        for j in range(4):
            left_ref[row : row + 64, 128 * j : 128 * j + 128] = halves(tiles[2 * j], tiles[2 * j + 1], right)
        for side, ref in enumerate((pair_ref, other_ref)):
            tile = ref[64 * band : 64 * band + 64]
            if lane_group:
                tile = pltpu.roll(tile, 128 - 32 * lane_group, 1)
            left_ref[row : row + 64, 512 + 128 * side : 640 + 128 * side] = tile

    for a, ref in enumerate((x_ref, g_ref)):
        for t in range(4):
            tiles = [ref[s, :, 128 * t : 128 * t + 128] for s in range(8)]
            for parity in range(2):
                fill(512 * a + 64 * (2 * t + parity), tiles, parity, t, 2 * parity + a)
    for side, ref in enumerate((below_ref, above_ref)):
        tiles = [ref[s] for s in range(8)]
        for a in range(2):
            fill(1024 + 128 * side + 64 * a, tiles, a, 4, 2 * side + a)

    for a in range(2):
        planes_ref[640 * a + 64 : 640 * a + 576] = jnp.dot(
            left_ref[512 * a : 512 * a + 512], place_ref[1], preferred_element_type=F32
        ).astype(BF)
    for side in range(2):
        both = jnp.dot(
            left_ref[1024 + 128 * side : 1152 + 128 * side],
            place_ref[2 * side],
            preferred_element_type=F32,
        ).astype(BF)
        planes_ref[576 * side : 576 * side + 64] = both[:64]
        planes_ref[640 + 576 * side : 640 + 576 * side + 64] = both[64:]

    total_ref[...] = jnp.zeros_like(total_ref)
    lane = iota((64, 128), 1)
    column = lane % 10
    inner = (lane >= 10) & (lane < 90) & (column >= 1) & (column <= 8)

    def step(slot, carry):
        at = pl.ds(pl.multiple_of(slot * 128, 128), 128)
        own = [
            jnp.where(inner, planes_ref[640 + 64 * (z + 1) : 704 + 64 * (z + 1), at], jnp.zeros((), BF))
            for z in range(8)
        ]
        moved = jnp.concatenate(
            [
                jnp.concatenate([pltpu.roll(o, shift % 128, 1) if shift else o for o in own], axis=1)
                for shift in SHIFTS
            ],
            axis=0,
        )
        total_ref[...] += lax.dot_general(
            moved, taps(planes_ref, slot, 0, 8), (((1,), (1,)), ((), ())), preferred_element_type=F32
        )
        return carry

    lax.fori_loop(0, 8, step, 0)
    scale = scale_ref[0]

    def part(k):
        if k == 27:
            return jnp.zeros((64, 64), F32)
        return total_ref[64 * (k % 9) : 64 * (k % 9) + 64, 64 * (k // 9) : 64 * (k // 9) + 64] * scale

    for j in range(14):
        terms_ref[64 * j : 64 * j + 64] = jnp.concatenate([part(2 * j), part(2 * j + 1)], axis=1)


def planes_and_terms(scale, place, x, g, below, above, pair, other):
    vmem = pl.BlockSpec(memory_space=pltpu.VMEM)
    return pl.pallas_call(
        terms_kernel,
        in_specs=[pl.BlockSpec(memory_space=pltpu.SMEM)] + [vmem] * 7,
        out_specs=[vmem, vmem],
        out_shape=[
            jax.ShapeDtypeStruct((1280, 1024), BF),
            jax.ShapeDtypeStruct((896, 128), F32),
        ],
        scratch_shapes=[pltpu.VMEM((1280, 768), BF), pltpu.VMEM((576, 192), F32)],
        compiler_params=params(),
        cost_estimate=pl.CostEstimate(flops=10**10, bytes_accessed=10**7, transcendentals=0),
        name="terms",
    )(scale, place, x, g, below, above, pair, other)


def conv_kernel(planes_ref, weight_ref, out_ref):
    row = iota((256, 128), 0)
    lane = row % 128
    y, x = lane // 10 - 1, lane % 10 - 1
    inner = (y >= 0) & (y < 8) & (x >= 0) & (x < 8)
    pick = jnp.where(
        inner & (iota((256, 128), 1) == (row // 128) * 64 + y * 8 + x), 1.0, 0.0
    ).astype(BF)

    def step(slot, carry):
        for zp in range(4):
            parts = jnp.dot(weight_ref[...], taps(planes_ref, slot, 2 * zp, 2), preferred_element_type=F32)
            tiles = []
            for h in range(2):
                total = None
                for m, shift in enumerate(SHIFTS):
                    piece = parts[64 * m : 64 * m + 64, 128 * h : 128 * h + 128]
                    if shift:
                        piece = pltpu.roll(piece, (-shift) % 128, 1)
                    total = piece if total is None else total + piece
                tiles.append(total.astype(BF))
            out_ref[slot, :, 128 * zp : 128 * zp + 128] = jnp.dot(
                jnp.concatenate(tiles, axis=1), pick, preferred_element_type=F32
            ).astype(BF)
        return carry

    lax.fori_loop(0, 8, step, 0)


def conv(planes, weight, which):
    return pl.pallas_call(
        conv_kernel,
        grid=(1,),
        in_specs=[
            pl.BlockSpec((640, 1024), lambda i: (which, 0)),
            pl.BlockSpec((576, 192), lambda i: (0, 0)),
        ],
        out_specs=pl.BlockSpec((8, 64, 512), lambda i: (0, 0, 0)),
        out_shape=jax.ShapeDtypeStruct((8, 64, 512), BF),
        compiler_params=params(),
        cost_estimate=pl.CostEstimate(flops=5 * 10**9, bytes_accessed=10**7, transcendentals=0),
        name="conv",
    )(planes, weight)


def coords(i):
    t = i % 64
    return [i // 64, t // 16, (t // 8) % 2, (t // 2) % 4, t % 2]


AXIS = {"zl": (0, 4), "y": (1, 4), "zh": (2, 2), "x": (3, 4), "c": (4, 2)}


def shift_pairs(key, by):
    at, size = AXIS[key]
    out = []
    for i in range(N_DEV):
        v = coords(i)
        v[at] = (v[at] + by) % size
        out.append((i, v[0] * 64 + ((v[1] * 2 + v[2]) * 4 + v[3]) * 2 + v[4]))
    return out


def send(x, key, by):
    return lax.ppermute(x, AXES, shift_pairs(key, by))


def scatter_sum(x, key, me):
    size = AXIS[key][1]
    parts = x.reshape(size, -1, x.shape[-1])
    total = lax.dynamic_index_in_dim(parts, me, 0, False)
    for s in range(1, size):
        total = total + send(lax.dynamic_index_in_dim(parts, (me + s) % size, 0, False), key, s)
    return total


def full_sum(x, key):
    total = x
    for s in range(1, AXIS[key][1]):
        total = total + send(x, key, s)
    return total


def gather(x, key, me):
    size = AXIS[key][1]
    found = jnp.stack([x] + [send(x, key, -s) for s in range(1, size)])
    return jnp.concatenate(
        [lax.dynamic_index_in_dim(found, (j - me) % size, 0, False) for j in range(size)], axis=0
    )


def total_over_devices(terms, slab, tile):
    core, x = tile % 2, (tile // 2) % 4
    part = scatter_sum(terms, "c", core)
    part = scatter_sum(part, "x", x)
    part = full_sum(part, "y")
    part = full_sum(part, "zl")
    part = full_sum(part, "zh")
    part = gather(part, "x", x)
    return gather(part, "c", core)


def shards(features, cotangent, weight, block_table):
    slab = lax.axis_index("slab")
    tile = lax.axis_index("tile")
    core = (tile % 2).astype(jnp.int32).reshape(1)
    table = jnp.pad(block_table, ((1, 1), (1, 1), (0, 0)), constant_values=-1)
    window = lax.dynamic_slice(table, (slab, tile * YR, 0), (3, 4, LX)).reshape(96)
    voxels = jnp.sum((block_table >= 0).astype(F32)) * 512.0
    scale = (1.0 / jnp.sqrt(voxels)).reshape(1)

    low, high = faces(features, cotangent)
    below = lax.ppermute(high, "slab", [(0, 1), (1, 2), (2, 3)])
    above = lax.ppermute(low, "slab", [(1, 0), (2, 1), (3, 2)])
    to_pair, to_other = edges(core, features, cotangent, below, above)
    pair = lax.ppermute(to_pair, "tile", [(i, i ^ 1) for i in range(64)])
    swaps = [(i, i + 1) for i in range(1, 63, 2)]
    other = lax.ppermute(to_other, "tile", swaps + [(b, a) for a, b in swaps])
    place = places(core, window)

    planes, terms = planes_and_terms(scale, place, features, cotangent, below, above, pair, other)
    spread = weight.reshape(64, 3, 9, 64)
    forward = spread.transpose(2, 0, 1, 3).reshape(576, 192)
    backward = spread[:, ::-1, ::-1].transpose(2, 3, 1, 0).reshape(576, 192)
    conv_out = conv(planes, forward, 0)
    grad_features = conv(planes, backward, 1)
    summed = total_over_devices(terms, slab, tile)
    grad_weight = summed.reshape(14, 64, 128).transpose(1, 0, 2).reshape(64, 1792)[:, :1728]
    return conv_out, grad_features, grad_weight


def solution(mesh):
    rows = P(AXES, None, None)
    return jax.shard_map(
        shards,
        mesh=mesh,
        in_specs=(rows, rows, P(), P()),
        out_specs=(rows, rows, P()),
        check_vma=False,
    )
```

profile of v0, /device:TPU:1, one launch (start us, length us, event | category | flops | bytes accessed | tf_op | source)
XLA Modules:
  0.0 114.2 jit_solution(11524038983977390490)
XLA Ops:
  0.6 1.0 copy-done.1
  1.7 1.0 copy-done.4
  2.9 4.5 %collective-permute-start = (bf16[8,64,128]{2,1,0:T(8,128)(2,1)S(1)}, bf16[8,64,128]{2,1,0:T(8,128)(2,1)S(1)}, u32[]{:S(2)}, u32[]{:S(2)}) collective-permute-start(bf16[8,64,128]{2,1,0:T(8,128)(2,1)S(1)} %get-tuple-element.9), channel_id=1, source_target_pairs={{0,64},{64,128},{128,192},{1,65},{65,129},{129,193},{2,66},{66,130... | collective-permute-start | bytes 393224 | tf_op jit(solution)/shard_map/ppermute | solution.py:365
  7.4 1.3 %collective-permute-start.1 = (bf16[8,64,128]{2,1,0:T(8,128)(2,1)S(1)}, bf16[8,64,128]{2,1,0:T(8,128)(2,1)S(1)}, u32[]{:S(2)}, u32[]{:S(2)}) collective-permute-start(bf16[8,64,128]{2,1,0:T(8,128)(2,1)S(1)} %get-tuple-element.10), channel_id=1, source_target_pairs={{64,0},{128,64},{192,128},{65,1},{129,65},{193,129},{66,2},{130,66... | collective-permute-start | bytes 393224 | tf_op jit(solution)/shard_map/ppermute | solution.py:366
  8.7 1.3 %convert_reduce_fusion = f32[]{:T(128)} fusion(s32[4,128,8]{1,2,0:T(8,128)} %param.7), kind=kLoop, calls=%fused_computation.28 | loop fusion | flops 12287 | bytes 16388 | tf_op jit(solution)/shard_map/reduce_sum | solution.py:361
  10.7 3.0 %collective-permute-done.1.above_ref = bf16[8,64,128]{2,1,0:T(8,128)(2,1)S(1)} collective-permute-done((bf16[8,64,128]{2,1,0:T(8,128)(2,1)S(1)}, bf16[8,64,128]{2,1,0:T(8,128)(2,1)S(1)}, u32[]{:S(2)}, u32[]{:S(2)}) %collective-permute-start.1) | collective-permute-done | bytes 131104 | tf_op jit(solution)/shard_map/ppermute | solution.py:366
  13.7 1.0 copy-done.2
  14.8 1.0 copy-done.5
  16.8 1.8 %collective-permute-start.2 = (bf16[320,128]{1,0:T(8,128)(2,1)S(1)}, bf16[320,128]{1,0:T(8,128)(2,1)S(1)}, u32[]{:S(2)}, u32[]{:S(2)}) collective-permute-start(bf16[320,128]{1,0:T(8,128)(2,1)S(1)} %get-tuple-element.11), channel_id=1, source_target_pairs={{0,1},{1,0},{2,3},{3,2},{4,5},{5,4},{6,7},{7,6},{8,9},{9,8},{10,11... | collective-permute-start | bytes 245768 | tf_op jit(solution)/shard_map/ppermute | solution.py:368
  18.5 3.0 %collective-permute-start.3 = (bf16[320,128]{1,0:T(8,128)(2,1)S(1)}, bf16[320,128]{1,0:T(8,128)(2,1)S(1)}, u32[]{:S(2)}, u32[]{:S(2)}) collective-permute-start(bf16[320,128]{1,0:T(8,128)(2,1)S(1)} %get-tuple-element.12), channel_id=1, source_target_pairs={{1,2},{3,4},{5,6},{7,8},{9,10},{11,12},{13,14},{15,16},{17,18},{19... | collective-permute-start | bytes 245768 | tf_op jit(solution)/shard_map/ppermute | solution.py:370
  22.5 1.9 %places.1.place_ref = bf16[3,768,1024]{2,1,0:T(8,128)(2,1)S(1)} custom-call(s32[1]{0:T(128)} %bitcast.1.core_ref, s32[96]{0:T(128)S(1)} %reshape.38.table_ref), custom_call_target="tpu_custom_call" | custom-call | tf_op jit(solution)/shard_map/places/pallas_call | solution.py:144
  24.5 2.1 %copy-done = bf16[3,768,1024]{2,1,0:T(8,128)(2,1)} copy-done((bf16[3,768,1024]{2,1,0:T(8,128)(2,1)}, bf16[3,768,1024]{2,1,0:T(8,128)(2,1)S(1)}, u32[]{:S(2)}) %copy-start) | copy-done | bytes 4718616
  26.7 9.1 %terms.1 = (bf16[1280,1024]{1,0:T(8,128)(2,1)S(1)}, f32[896,128]{1,0:T(8,128)S(1)}) custom-call(f32[1]{0:T(128)} %bitcast.scale_ref, bf16[3,768,1024]{2,1,0:T(8,128)(2,1)} %copy-done, bf16[8,64,512]{2,1,0:T(8,128)(2,1)S(1)} %copy-done.3, bf16[8,64,512]{2,1,0:T(8,128)(2,1)S(1)} %copy-done.6, bf16[8,64,128]{2,1,0:T(8,128)(2,1)S(1)} %collective-permute-done.below_ref, ...), custom_call_target="tpu_custom_call" | custom-call | flops 10000000000 | bytes 10000000 | tf_op jit(solution)/shard_map/terms/pallas_call | solution.py:238
  35.7 1.5 %copy-done.7 = bf16[1280,1024]{1,0:T(8,128)(2,1)} copy-done((bf16[1280,1024]{1,0:T(8,128)(2,1)}, bf16[1280,1024]{1,0:T(8,128)(2,1)S(1)}, u32[]{:S(2)}) %copy-start.7) | copy-done | bytes 2621464
  37.4 1.4 %collective-permute-done.4 = f32[448,128]{1,0:T(8,128)S(1)} collective-permute-done((f32[448,128]{1,0:T(8,128)S(1)}, f32[448,128]{1,0:T(8,128)S(1)}, u32[]{:S(2)}, u32[]{:S(2)}) %collective-permute-start.4) | collective-permute-done | bytes 229408 | tf_op jit(solution)/shard_map/ppermute | solution.py:317
  38.9 7.1 %collective-permute-start.7 = (f32[112,128]{1,0:T(8,128)S(1)}, f32[112,128]{1,0:T(8,128)S(1)}, u32[]{:S(2)}, u32[]{:S(2)}) collective-permute-start(f32[112,128]{1,0:T(8,128)S(1)} %get-tuple-element.24), channel_id=1, source_target_pairs={{0,6},{1,7},{2,0},{3,1},{4,2},{5,3},{6,4},{7,5},{8,14},{9,15},{10,... | collective-permute-start | bytes 172040 | tf_op jit(solution)/shard_map/ppermute | solution.py:317
  47.3 3.4 %collective-permute-done.6 = f32[112,128]{1,0:T(8,128)S(1)} collective-permute-done((f32[112,128]{1,0:T(8,128)S(1)}, f32[112,128]{1,0:T(8,128)S(1)}, u32[]{:S(2)}, u32[]{:S(2)}) %collective-permute-start.6) | collective-permute-done | bytes 57376 | tf_op jit(solution)/shard_map/ppermute | solution.py:317
  50.6 1.1 collective-permute-done.5
  51.7 3.6 %collective-permute-start.10 = (f32[112,128]{1,0:T(8,128)S(1)}, f32[112,128]{1,0:T(8,128)S(1)}, u32[]{:S(2)}, u32[]{:S(2)}) collective-permute-start(f32[112,128]{1,0:T(8,128)S(1)} %fusion.5), channel_id=1, source_target_pairs={{0,48},{1,49},{2,50},{3,51},{4,52},{5,53},{6,54},{7,55},{8,56},{9,... | collective-permute-start | bytes 172040 | tf_op jit(solution)/shard_map/ppermute | solution.py:317
  56.6 3.4 %collective-permute-done.9 = f32[112,128]{1,0:T(8,128)S(1)} collective-permute-done((f32[112,128]{1,0:T(8,128)S(1)}, f32[112,128]{1,0:T(8,128)S(1)}, u32[]{:S(2)}, u32[]{:S(2)}) %collective-permute-start.9) | collective-permute-done | bytes 57376 | tf_op jit(solution)/shard_map/ppermute | solution.py:317
  61.2 1.7 %collective-permute-start.12 = (f32[112,128]{1,0:T(8,128)S(1)}, f32[112,128]{1,0:T(8,128)S(1)}, u32[]{:S(2)}, u32[]{:S(2)}) collective-permute-start(f32[112,128]{1,0:T(8,128)S(1)} %add_add_fusion.1), channel_id=1, source_target_pairs={{0,128},{1,129},{2,130},{3,131},{4,132},{5,133},{6,134},{7,135},{8... | collective-permute-start | bytes 172040 | tf_op jit(solution)/shard_map/ppermute | solution.py:317
  64.0 1.1 collective-permute-done.12
  65.2 3.2 %collective-permute-done.11 = f32[112,128]{1,0:T(8,128)} collective-permute-done((f32[112,128]{1,0:T(8,128)S(1)}, f32[112,128]{1,0:T(8,128)}, u32[]{:S(2)}, u32[]{:S(2)}) %collective-permute-start.11) | collective-permute-done | bytes 57376 | tf_op jit(solution)/shard_map/ppermute | solution.py:317
  69.2 4.5 %collective-permute-start.14 = (f32[112,128]{1,0:T(8,128)S(1)}, f32[112,128]{1,0:T(8,128)S(1)}, u32[]{:S(2)}, u32[]{:S(2)}) collective-permute-start(f32[112,128]{1,0:T(8,128)S(1)} %add_add_fusion), channel_id=1, source_target_pairs={{0,8},{1,9},{2,10},{3,11},{4,12},{5,13},{6,14},{7,15},{8,0},{9,1},... | collective-permute-start | bytes 172040 | tf_op jit(solution)/shard_map/ppermute | solution.py:317
  74.5 1.3 %copy.12 = bf16[9,64,3,64]{3,2,1,0:T(4,128)(2,1)} copy(bf16[9,64,3,64]{1,3,0,2:T(8,128)(2,1)S(1)} %bitcast.55) | data formatting | bytes 442368 | tf_op jit(solution)/shard_map/transpose | solution.py:375
  75.8 1.5 %reshape.40.weight_ref = bf16[576,192]{1,0:T(8,128)(2,1)S(1)} reshape(bf16[9,64,3,64]{3,2,1,0:T(4,128)(2,1)} %copy.12) | data formatting | bytes 442368 | tf_op jit(solution)/shard_map/reshape | solution.py:375
  77.4 2.2 %copy.13 = bf16[9,64,3,64]{3,2,1,0:T(4,128)(2,1)} copy(bf16[9,64,3,64]{3,1,0,2:T(8,128)(2,1)} %reverse_bitcast_fusion) | data formatting | bytes 442368 | tf_op jit(solution)/shard_map/transpose | solution.py:376
  79.6 1.5 %reshape.41.weight_ref = bf16[576,192]{1,0:T(8,128)(2,1)S(1)} reshape(bf16[9,64,3,64]{3,2,1,0:T(4,128)(2,1)} %copy.13) | data formatting | bytes 442368 | tf_op jit(solution)/shard_map/reshape | solution.py:376
  81.3 1.9 %collective-permute-start.16 = (f32[112,128]{1,0:T(8,128)S(1)}, f32[112,128]{1,0:T(8,128)S(1)}, u32[]{:S(2)}, u32[]{:S(2)}) collective-permute-start(f32[112,128]{1,0:T(8,128)S(1)} %add.158), channel_id=1, source_target_pairs={{0,4},{1,5},{2,6},{3,7},{4,0},{5,1},{6,2},{7,3},{8,12},{9,13},{10,... | collective-permute-start | bytes 172040 | tf_op jit(solution)/shard_map/ppermute | solution.py:317
  84.0 11.8 %conv.2 = bf16[8,64,512]{2,1,0:T(8,128)(2,1)} custom-call(bf16[1280,1024]{1,0:T(8,128)(2,1)S(1)} %copy-done.8, bf16[576,192]{1,0:T(8,128)(2,1)S(1)} %reshape.40.weight_ref), custom_call_target="tpu_custom_call" | custom-call | flops 5000000000 | bytes 10000000 | tf_op jit(solution)/shard_map/conv/pallas_call | solution.py:283
  95.8 5.6 %collective-permute-start.18 = (f32[448,128]{1,0:T(8,128)S(1)}, f32[448,128]{1,0:T(8,128)S(1)}, u32[]{:S(2)}, u32[]{:S(2)}) collective-permute-start(f32[448,128]{1,0:T(8,128)S(1)} %get-tuple-element.17), channel_id=1, source_target_pairs={{0,1},{1,0},{2,3},{3,2},{4,5},{5,4},{6,7},{7,6},{8,9},{9,8},{10,11... | collective-permute-start | bytes 688136 | tf_op jit(solution)/shard_map/ppermute | solution.py:317
  101.5 11.8 %conv.3 = bf16[8,64,512]{2,1,0:T(8,128)(2,1)} custom-call(bf16[1280,1024]{1,0:T(8,128)(2,1)S(1)} %copy-done.8, bf16[576,192]{1,0:T(8,128)(2,1)S(1)} %reshape.41.weight_ref), custom_call_target="tpu_custom_call" | custom-call | flops 5000000000 | bytes 10000000 | tf_op jit(solution)/shard_map/conv/pallas_call | solution.py:283
  (55 shorter events, 10.7 us)
Async XLA Ops:
  0.6 1.0 copy-start.1
  1.7 1.0 copy-start.4
  2.7 23.9 %copy-start.3 = (bf16[8,64,512]{2,1,0:T(8,128)(2,1)S(1)}, bf16[8,64,512]{2,1,0:T(8,128)(2,1)}, u32[]{:S(2)}) copy-start(bf16[8,64,512]{2,1,0:T(8,128)(2,1)} %x_ref.3) | copy-start | bytes 1572868
  2.7 23.9 %copy-start.6 = (bf16[8,64,512]{2,1,0:T(8,128)(2,1)S(1)}, bf16[8,64,512]{2,1,0:T(8,128)(2,1)}, u32[]{:S(2)}) copy-start(bf16[8,64,512]{2,1,0:T(8,128)(2,1)} %g_ref.3) | copy-start | bytes 1572868
  2.9 7.9 %collective-permute-start = (bf16[8,64,128]{2,1,0:T(8,128)(2,1)S(1)}, bf16[8,64,128]{2,1,0:T(8,128)(2,1)S(1)}, u32[]{:S(2)}, u32[]{:S(2)}) collective-permute-start(bf16[8,64,128]{2,1,0:T(8,128)(2,1)S(1)} %get-tuple-element.9), channel_id=1, source_target_pairs={{0,64},{64,128},{128,192},{1,65},{65,129},{129,193},{2,66},{66,130... | collective-permute-start | bytes 393224 | tf_op jit(solution)/shard_map/ppermute | solution.py:365
  7.4 6.3 %collective-permute-start.1 = (bf16[8,64,128]{2,1,0:T(8,128)(2,1)S(1)}, bf16[8,64,128]{2,1,0:T(8,128)(2,1)S(1)}, u32[]{:S(2)}, u32[]{:S(2)}) collective-permute-start(bf16[8,64,128]{2,1,0:T(8,128)(2,1)S(1)} %get-tuple-element.10), channel_id=1, source_target_pairs={{64,0},{128,64},{192,128},{65,1},{129,65},{193,129},{66,2},{130,66... | collective-permute-start | bytes 393224 | tf_op jit(solution)/shard_map/ppermute | solution.py:366
  13.7 1.0 copy-start.2
  14.8 1.0 copy-start.5
  16.8 9.9 %collective-permute-start.2 = (bf16[320,128]{1,0:T(8,128)(2,1)S(1)}, bf16[320,128]{1,0:T(8,128)(2,1)S(1)}, u32[]{:S(2)}, u32[]{:S(2)}) collective-permute-start(bf16[320,128]{1,0:T(8,128)(2,1)S(1)} %get-tuple-element.11), channel_id=1, source_target_pairs={{0,1},{1,0},{2,3},{3,2},{4,5},{5,4},{6,7},{7,6},{8,9},{9,8},{10,11... | collective-permute-start | bytes 245768 | tf_op jit(solution)/shard_map/ppermute | solution.py:368
  18.5 8.1 %collective-permute-start.3 = (bf16[320,128]{1,0:T(8,128)(2,1)S(1)}, bf16[320,128]{1,0:T(8,128)(2,1)S(1)}, u32[]{:S(2)}, u32[]{:S(2)}) collective-permute-start(bf16[320,128]{1,0:T(8,128)(2,1)S(1)} %get-tuple-element.12), channel_id=1, source_target_pairs={{1,2},{3,4},{5,6},{7,8},{9,10},{11,12},{13,14},{15,16},{17,18},{19... | collective-permute-start | bytes 245768 | tf_op jit(solution)/shard_map/ppermute | solution.py:370
  24.5 2.1 %copy-start = (bf16[3,768,1024]{2,1,0:T(8,128)(2,1)}, bf16[3,768,1024]{2,1,0:T(8,128)(2,1)S(1)}, u32[]{:S(2)}) copy-start(bf16[3,768,1024]{2,1,0:T(8,128)(2,1)S(1)} %places.1.place_ref) | copy-start | bytes 14155780
  26.7 37.1 %copy-start.9 = (bf16[64,1728]{1,0:T(8,128)(2,1)S(1)}, bf16[64,1728]{1,0:T(8,128)(2,1)}, u32[]{:S(2)}) copy-start(bf16[64,1728]{1,0:T(8,128)(2,1)} %param.6) | copy-start | bytes 663556
  35.7 1.5 %copy-start.7 = (bf16[1280,1024]{1,0:T(8,128)(2,1)}, bf16[1280,1024]{1,0:T(8,128)(2,1)S(1)}, u32[]{:S(2)}) copy-start(bf16[1280,1024]{1,0:T(8,128)(2,1)S(1)} %get-tuple-element.13.planes_ref) | copy-start | bytes 7864324
  37.3 1.6 %collective-permute-start.4 = (f32[448,128]{1,0:T(8,128)S(1)}, f32[448,128]{1,0:T(8,128)S(1)}, u32[]{:S(2)}, u32[]{:S(2)}) collective-permute-start(f32[448,128]{1,0:T(8,128)S(1)} %dynamic-slice_bitcast_fusion), channel_id=1, source_target_pairs={{0,1},{1,0},{2,3},{3,2},{4,5},{5,4},{6,7},{7,6},{8,9},{9,8},{10,11... | collective-permute-start | bytes 688136 | tf_op jit(solution)/shard_map/ppermute | solution.py:317
  38.9 45.1 %copy-start.8 = (bf16[1280,1024]{1,0:T(8,128)(2,1)S(1)}, bf16[1280,1024]{1,0:T(8,128)(2,1)}, u32[]{:S(2)}) copy-start(bf16[1280,1024]{1,0:T(8,128)(2,1)} %copy-done.7) | copy-start | bytes 7864324
  38.9 8.4 %collective-permute-start.7 = (f32[112,128]{1,0:T(8,128)S(1)}, f32[112,128]{1,0:T(8,128)S(1)}, u32[]{:S(2)}, u32[]{:S(2)}) collective-permute-start(f32[112,128]{1,0:T(8,128)S(1)} %get-tuple-element.24), channel_id=1, source_target_pairs={{0,6},{1,7},{2,0},{3,1},{4,2},{5,3},{6,4},{7,5},{8,14},{9,15},{10,... | collective-permute-start | bytes 172040 | tf_op jit(solution)/shard_map/ppermute | solution.py:317
  46.0 4.6 %collective-permute-start.6 = (f32[112,128]{1,0:T(8,128)S(1)}, f32[112,128]{1,0:T(8,128)S(1)}, u32[]{:S(2)}, u32[]{:S(2)}) collective-permute-start(f32[112,128]{1,0:T(8,128)S(1)} %get-tuple-element.25), channel_id=1, source_target_pairs={{0,4},{1,5},{2,6},{3,7},{4,0},{5,1},{6,2},{7,3},{8,12},{9,13},{10,... | collective-permute-start | bytes 172040 | tf_op jit(solution)/shard_map/ppermute | solution.py:317
  46.0 5.7 %collective-permute-start.5 = (f32[112,128]{1,0:T(8,128)S(1)}, f32[112,128]{1,0:T(8,128)S(1)}, u32[]{:S(2)}, u32[]{:S(2)}) collective-permute-start(f32[112,128]{1,0:T(8,128)S(1)} %get-tuple-element.23), channel_id=1, source_target_pairs={{0,2},{1,3},{2,4},{3,5},{4,6},{5,7},{6,0},{7,1},{8,10},{9,11},{10,... | collective-permute-start | bytes 172040 | tf_op jit(solution)/shard_map/ppermute | solution.py:317
  51.7 4.9 %collective-permute-start.10 = (f32[112,128]{1,0:T(8,128)S(1)}, f32[112,128]{1,0:T(8,128)S(1)}, u32[]{:S(2)}, u32[]{:S(2)}) collective-permute-start(f32[112,128]{1,0:T(8,128)S(1)} %fusion.5), channel_id=1, source_target_pairs={{0,48},{1,49},{2,50},{3,51},{4,52},{5,53},{6,54},{7,55},{8,56},{9,... | collective-permute-start | bytes 172040 | tf_op jit(solution)/shard_map/ppermute | solution.py:317
  55.4 4.6 %collective-permute-start.9 = (f32[112,128]{1,0:T(8,128)S(1)}, f32[112,128]{1,0:T(8,128)S(1)}, u32[]{:S(2)}, u32[]{:S(2)}) collective-permute-start(f32[112,128]{1,0:T(8,128)S(1)} %fusion.5), channel_id=1, source_target_pairs={{0,32},{1,33},{2,34},{3,35},{4,36},{5,37},{6,38},{7,39},{8,40},{9,... | collective-permute-start | bytes 172040 | tf_op jit(solution)/shard_map/ppermute | solution.py:317
  55.4 4.9 %collective-permute-start.8 = (f32[112,128]{1,0:T(8,128)S(1)}, f32[112,128]{1,0:T(8,128)S(1)}, u32[]{:S(2)}, u32[]{:S(2)}) collective-permute-start(f32[112,128]{1,0:T(8,128)S(1)} %fusion.5), channel_id=1, source_target_pairs={{0,16},{1,17},{2,18},{3,19},{4,20},{5,21},{6,22},{7,23},{8,24},{9,... | collective-permute-start | bytes 172040 | tf_op jit(solution)/shard_map/ppermute | solution.py:317
  60.3 3.7 %collective-permute-start.13 = (f32[112,128]{1,0:T(8,128)S(1)}, f32[112,128]{1,0:T(8,128)S(1)}, u32[]{:S(2)}, u32[]{:S(2)}) collective-permute-start(f32[112,128]{1,0:T(8,128)S(1)} %add_add_fusion.1), channel_id=1, source_target_pairs={{0,192},{1,193},{2,194},{3,195},{4,196},{5,197},{6,198},{7,199},{8... | collective-permute-start | bytes 172040 | tf_op jit(solution)/shard_map/ppermute | solution.py:317
  61.2 3.9 %collective-permute-start.12 = (f32[112,128]{1,0:T(8,128)S(1)}, f32[112,128]{1,0:T(8,128)S(1)}, u32[]{:S(2)}, u32[]{:S(2)}) collective-permute-start(f32[112,128]{1,0:T(8,128)S(1)} %add_add_fusion.1), channel_id=1, source_target_pairs={{0,128},{1,129},{2,130},{3,131},{4,132},{5,133},{6,134},{7,135},{8... | collective-permute-start | bytes 172040 | tf_op jit(solution)/shard_map/ppermute | solution.py:317
  62.9 5.4 %collective-permute-start.11 = (f32[112,128]{1,0:T(8,128)S(1)}, f32[112,128]{1,0:T(8,128)}, u32[]{:S(2)}, u32[]{:S(2)}) collective-permute-start(f32[112,128]{1,0:T(8,128)S(1)} %add_add_fusion.1), channel_id=1, source_target_pairs={{0,64},{1,65},{2,66},{3,67},{4,68},{5,69},{6,70},{7,71},{8,72},{9,... | collective-permute-start | bytes 172040 | tf_op jit(solution)/shard_map/ppermute | solution.py:317
  69.2 12.0 %collective-permute-start.14 = (f32[112,128]{1,0:T(8,128)S(1)}, f32[112,128]{1,0:T(8,128)S(1)}, u32[]{:S(2)}, u32[]{:S(2)}) collective-permute-start(f32[112,128]{1,0:T(8,128)S(1)} %add_add_fusion), channel_id=1, source_target_pairs={{0,8},{1,9},{2,10},{3,11},{4,12},{5,13},{6,14},{7,15},{8,0},{9,1},... | collective-permute-start | bytes 172040 | tf_op jit(solution)/shard_map/ppermute | solution.py:317
  81.2 14.6 %collective-permute-start.17 = (f32[112,128]{1,0:T(8,128)S(1)}, f32[112,128]{1,0:T(8,128)S(1)}, u32[]{:S(2)}, u32[]{:S(2)}) collective-permute-start(f32[112,128]{1,0:T(8,128)S(1)} %add.158), channel_id=1, source_target_pairs={{0,2},{1,3},{2,4},{3,5},{4,6},{5,7},{6,0},{7,1},{8,10},{9,11},{10,... | collective-permute-start | bytes 172040 | tf_op jit(solution)/shard_map/ppermute | solution.py:317
  81.3 14.5 %collective-permute-start.16 = (f32[112,128]{1,0:T(8,128)S(1)}, f32[112,128]{1,0:T(8,128)S(1)}, u32[]{:S(2)}, u32[]{:S(2)}) collective-permute-start(f32[112,128]{1,0:T(8,128)S(1)} %add.158), channel_id=1, source_target_pairs={{0,4},{1,5},{2,6},{3,7},{4,0},{5,1},{6,2},{7,3},{8,12},{9,13},{10,... | collective-permute-start | bytes 172040 | tf_op jit(solution)/shard_map/ppermute | solution.py:317
  83.2 12.5 %collective-permute-start.15 = (f32[112,128]{1,0:T(8,128)S(1)}, f32[112,128]{1,0:T(8,128)S(1)}, u32[]{:S(2)}, u32[]{:S(2)}) collective-permute-start(f32[112,128]{1,0:T(8,128)S(1)} %add.158), channel_id=1, source_target_pairs={{0,6},{1,7},{2,0},{3,1},{4,2},{5,3},{6,4},{7,5},{8,14},{9,15},{10,... | collective-permute-start | bytes 172040 | tf_op jit(solution)/shard_map/ppermute | solution.py:317
  95.8 17.4 %collective-permute-start.18 = (f32[448,128]{1,0:T(8,128)S(1)}, f32[448,128]{1,0:T(8,128)S(1)}, u32[]{:S(2)}, u32[]{:S(2)}) collective-permute-start(f32[448,128]{1,0:T(8,128)S(1)} %get-tuple-element.17), channel_id=1, source_target_pairs={{0,1},{1,0},{2,3},{3,2},{4,5},{5,4},{6,7},{7,6},{8,9},{9,8},{10,11... | collective-permute-start | bytes 688136 | tf_op jit(solution)/shard_map/ppermute | solution.py:317
where the time goes:
time: 115 us; the launch traced here: 114 us
  starting transfers between devices  39.2 us (34%)
  Pallas kernels  35.6 us (31%)
  waiting for transfers between devices  17.8 us (15%)
  local copies, waits for them, and re-layouts  17.3 us (15%)
  other arithmetic  2.41 us (2%)
  between operations  1.72 us (1%)
    ppermute x15, starting transfers between devices, send(): return lax.ppermute(x, AXES, shift_pairs(key, by))  28.7 us
    pallas_call x2, Pallas kernels, conv(): pl.pallas_call(conv_kernel, grid=(1,), in_specs=[pl.BlockSpec((640, 1024)...  23.5 us
    ppermute x15, waiting for transfers between devices, send(): return lax.ppermute(x, AXES, shift_pairs(key, by))  14.9 us
    pallas_call x1, Pallas kernels, planes_and_terms(): pl.pallas_call(terms_kernel, in_specs=[pl.BlockSpec(memory_space=pltpu.SM...  9.05 us
    unnamed x21, local copies, waits for them, and re-layouts  8.08 us
    ppermute x1, starting transfers between devices, shards(): below = lax.ppermute(high, 'slab', [(0, 1), (1, 2), (2, 3)])  4.51 us
    ppermute x1, starting transfers between devices, shards(): other = lax.ppermute(to_other, 'tile', swaps + [(b, a) for a, b in swaps])  3.02 us
    transpose x2, local copies, waits for them, and re-layouts, shards(): backward = spread[:, ::-1, ::-1].transpose(2, 3, 1, 0).reshape(576, 192)  3 us
  transfers between devices with their start and end apart: 19, of which 10 were waited for; matrix products, arithmetic and copies ran while one was open for 9% of the time, Pallas kernels for 22%

commit v1 on v0

v1 whole, which is shorter than its diff:
```python
import functools

import jax
import jax.numpy as jnp
from jax import lax
from jax.experimental import pallas as pl
from jax.experimental.pallas import tpu as pltpu
from jax.sharding import PartitionSpec as P

LX = 8
YR = 2
BF = jnp.bfloat16
F32 = jnp.float32
AXES = ("slab", "tile")
N_DEV = 256
VMEM_LIMIT = 24 * 1024 * 1024
SHIFTS = [dy * 10 + dx for dy in (-1, 0, 1) for dx in (-1, 0, 1)]


def params():
    return pltpu.CompilerParams(vmem_limit_bytes=VMEM_LIMIT)


def iota(shape, dim):
    return lax.broadcasted_iota(jnp.int32, shape, dim)


def halves(a, b, right):
    cut = slice(64, 128) if right else slice(0, 64)
    return jnp.concatenate([a[:, cut], b[:, cut]], axis=1)


def in_hbm(x):
    return pltpu.with_memory_space_constraint(x, pltpu.HBM)


def in_vmem(x):
    return pltpu.with_memory_space_constraint(x, pltpu.VMEM)


def faces_kernel(x_ref, g_ref, low_ref, high_ref, xv_ref, gv_ref, sems):
    copies = [
        pltpu.make_async_copy(src.at[4 * h : 4 * h + 4], dst.at[4 * h : 4 * h + 4], sems.at[2 * h + i])
        for h in range(2)
        for i, (src, dst) in enumerate(((x_ref, xv_ref), (g_ref, gv_ref)))
    ]
    for copy in copies:
        copy.start()
    for h in range(2):
        for copy in copies[2 * h : 2 * h + 2]:
            copy.wait()
        for s in range(4 * h, 4 * h + 4):
            low_ref[s] = halves(xv_ref[s, :, :128], gv_ref[s, :, :128], False)
            high_ref[s] = halves(xv_ref[s, :, 384:], gv_ref[s, :, 384:], True)


def faces(x, g):
    vmem = pl.BlockSpec(memory_space=pltpu.VMEM)
    hbm = pl.BlockSpec(memory_space=pltpu.HBM)
    face = jax.ShapeDtypeStruct((8, 64, 128), BF)
    held = pltpu.VMEM((8, 64, 512), BF)
    return pl.pallas_call(
        faces_kernel,
        in_specs=[hbm, hbm],
        out_specs=[vmem] * 4,
        out_shape=[face, face, held, held],
        scratch_shapes=[pltpu.SemaphoreType.DMA((4,))],
        compiler_params=params(),
        name="faces",
    )(in_hbm(x), in_hbm(g))


def edges_kernel(core_ref, window_ref, scale_ref, x_ref, g_ref, below_ref, above_ref, pair_ref, other_ref):
    chunk = iota((1024, 128), 0) // 128
    lane = iota((1024, 128), 0) % 128
    to = iota((1024, 128), 1)

    def picks(y):
        here = (lane // 8) % 8 == y
        edge = (lane // 64) * 64 + chunk * 8 + lane % 8
        line = (chunk // 4) * 64 + (lane // 64) * 32 + (chunk % 4) * 8 + lane % 8
        return [
            jnp.where(here & (at == to), 1.0, 0.0).astype(BF) for at in (edge, line)
        ]

    found = []
    for first, y in ((4, 7), (0, 0)):
        edge, line = picks(y)
        rows = [
            jnp.concatenate(
                [ref[first + s, :, 128 * t : 128 * t + 128] for ref in (x_ref, g_ref) for s in range(4)],
                axis=1,
            )
            for t in range(4)
        ]
        lines = jnp.concatenate(
            [ref[first + s] for ref in (below_ref, above_ref) for s in range(4)], axis=1
        )
        main = jnp.dot(jnp.concatenate(rows, axis=0), edge, preferred_element_type=F32)
        last = jnp.dot(lines, line, preferred_element_type=F32)
        found.append(jnp.concatenate([main, last], axis=0))
    up, down = found
    odd = core_ref[0]
    pair_ref[...] = jnp.where(odd == 0, up, down).astype(BF)
    other_ref[...] = jnp.where(odd == 0, down, up).astype(BF)


def edges(core, window, scale, x, g, below, above):
    out = jax.ShapeDtypeStruct((320, 128), BF)
    vmem = pl.BlockSpec(memory_space=pltpu.VMEM)
    return pl.pallas_call(
        edges_kernel,
        in_specs=[pl.BlockSpec(memory_space=pltpu.SMEM)] * 3 + [vmem] * 4,
        out_specs=[vmem, vmem],
        out_shape=[out, out],
        compiler_params=params(),
        name="edges",
    )(core, window, scale, x, g, below, above)


def prepare_kernel(core_ref, table_ref, weight_hbm, place_ref, forward_ref, backward_ref, weight_ref, sem):
    load = pltpu.make_async_copy(weight_hbm, weight_ref, sem)
    load.start()
    fill_places(core_ref, table_ref, place_ref)
    load.wait()
    rows = iota((128, 128), 0)
    same = jnp.where(rows == iota((128, 128), 1), 1.0, 0.0).astype(BF)
    for k in range(27):
        dz, m = k // 9, k % 9
        forward_ref[64 * m : 64 * m + 64, 64 * dz : 64 * dz + 64] = weight_ref[:, 64 * k : 64 * k + 64]
    for j in range(14):
        wide = min(128, 1728 - 128 * j)
        turned = lax.dot_general(
            same[:wide, :wide],
            weight_ref[:, 128 * j : 128 * j + wide],
            (((1,), (1,)), ((), ())),
            preferred_element_type=F32,
        ).astype(BF)
        for k in range(2 * j, 2 * j + wide // 64):
            dz, m = (26 - k) // 9, (26 - k) % 9
            backward_ref[64 * m : 64 * m + 64, 64 * dz : 64 * dz + 64] = turned[64 * (k - 2 * j) : 64 * (k - 2 * j) + 64]


def fill_places(core_ref, table_ref, place_ref):
    odd = core_ref[0]
    lane = iota((8, 128), 1)
    ly = lane // 10 - 1
    lx = lane % 10 - 1
    used = lane < 100
    y_class = jnp.where(ly < 0, 0, jnp.where(ly > 7, 2, 1))
    x_class = jnp.where(lx < 0, 0, jnp.where(lx > 7, 2, 1))
    near = jnp.where(used, y_class * 3 + x_class, -1)
    inner_x = lx & 7
    inner = (ly & 7) * 8 + inner_x
    rows = iota((768, 128), 0)
    for s in range(8):
        r = s // 4
        column = jnp.int32(-10)
        for b in range(8):
            column = jnp.where(table_ref[(4 + r + 1) * 8 + b] == s, b, column)
        for d in range(3):
            source = jnp.full((8, 128), -1, jnp.int32)
            for dy in range(3):
                row = r + dy
                for dx in range(3):
                    at = column + (dx - 1)
                    inside = (at >= 0) & (at < LX)
                    held = table_ref[(d * 4 + row) * 8 + jnp.clip(at, 0, LX - 1)]
                    fine = inside & (held >= 0)
                    if row in (1, 2):
                        base = jnp.where(fine, held * 64, -10000)
                        value = base + inner
                    else:
                        side = 1 - odd if row == 0 else odd
                        base = jnp.where(fine, 512 + side * 128 + (held & 3) * 8, -10000)
                        value = base + inner_x
                    source = jnp.where(near == dy * 3 + dx, value, source)
            place_ref[d, :, 128 * s : 128 * s + 128] = jnp.where(
                rows == source[0:1], 1.0, 0.0
            ).astype(BF)


def prepare(core, window, weight):
    smem = pl.BlockSpec(memory_space=pltpu.SMEM)
    vmem = pl.BlockSpec(memory_space=pltpu.VMEM)
    turned = pltpu.VMEM((576, 192), BF)
    return pl.pallas_call(
        prepare_kernel,
        in_specs=[smem, smem, pl.BlockSpec(memory_space=pltpu.HBM)],
        out_specs=[vmem] * 3,
        out_shape=[pltpu.VMEM((3, 768, 1024), BF), turned, turned],
        scratch_shapes=[pltpu.VMEM((64, 1728), BF), pltpu.SemaphoreType.DMA],
        compiler_params=params(),
        name="prepare",
    )(core, window, in_hbm(weight))


def taps(planes_ref, slot, z_from, z_count):
    at = slice(128 * slot, 128 * slot + 128)
    return jnp.concatenate(
        [
            jnp.concatenate(
                [planes_ref[64 * (z + dz) : 64 * (z + dz) + 64, at] for z in range(z_from, z_from + z_count)],
                axis=1,
            )
            for dz in range(3)
        ],
        axis=0,
    )


def terms_kernel(core_ref, scale_ref, place_ref, x_ref, g_ref, below_ref, above_ref, pair_ref, other_ref, x_planes_ref, g_planes_ref, mine_ref, theirs_ref, left_ref, total_ref, even_ref, odd_ref):
    def fill(row, tiles, right, band, lane_group):
        for j in range(4):
            left_ref[row : row + 64, 128 * j : 128 * j + 128] = halves(tiles[2 * j], tiles[2 * j + 1], right)
        for side, ref in enumerate((pair_ref, other_ref)):
            tile = ref[64 * band : 64 * band + 64]
            if lane_group:
                tile = pltpu.roll(tile, 128 - 32 * lane_group, 1)
            left_ref[row : row + 64, 512 + 128 * side : 640 + 128 * side] = tile

    for a, ref in enumerate((x_ref, g_ref)):
        for t in range(4):
            tiles = [ref[s, :, 128 * t : 128 * t + 128] for s in range(8)]
            for parity in range(2):
                fill(512 * a + 64 * (2 * t + parity), tiles, parity, t, 2 * parity + a)
    for side, ref in enumerate((below_ref, above_ref)):
        tiles = [ref[s] for s in range(8)]
        for a in range(2):
            fill(1024 + 128 * side + 64 * a, tiles, a, 4, 2 * side + a)

    for a, ref in enumerate((x_planes_ref, g_planes_ref)):
        ref[64:576] = jnp.dot(
            left_ref[512 * a : 512 * a + 512], place_ref[1], preferred_element_type=F32
        ).astype(BF)
    for side in range(2):
        both = jnp.dot(
            left_ref[1024 + 128 * side : 1152 + 128 * side],
            place_ref[2 * side],
            preferred_element_type=F32,
        ).astype(BF)
        x_planes_ref[576 * side : 576 * side + 64] = both[:64]
        g_planes_ref[576 * side : 576 * side + 64] = both[64:]

    total_ref[...] = jnp.zeros_like(total_ref)
    lane = iota((64, 128), 1)
    column = lane % 10
    inner = (lane >= 10) & (lane < 90) & (column >= 1) & (column <= 8)

    def move(slot, moved_ref):
        for z in range(8):
            at = slice(128 * slot, 128 * slot + 128)
            own = jnp.where(inner, g_planes_ref[64 * (z + 1) : 64 * (z + 1) + 64, at], jnp.zeros((), BF))
            for m, shift in enumerate(SHIFTS):
                moved_ref[64 * m : 64 * m + 64, 128 * z : 128 * z + 128] = (
                    pltpu.roll(own, shift % 128, 1) if shift else own
                )

    move(0, even_ref)
    for slot in range(8):
        now, later = (even_ref, odd_ref) if slot % 2 == 0 else (odd_ref, even_ref)
        if slot < 7:
            move(slot + 1, later)
        total_ref[...] += lax.dot_general(
            now[...], taps(x_planes_ref, slot, 0, 8), (((1,), (1,)), ((), ())), preferred_element_type=F32
        )
    scale = scale_ref[0]

    def part(k):
        if k == 27:
            return jnp.zeros((64, 64), F32)
        return total_ref[64 * (k % 9) : 64 * (k % 9) + 64, 64 * (k // 9) : 64 * (k // 9) + 64] * scale

    def write(refs):
        for j in range(14):
            at = 64 * (j % 7)
            refs[j // 7][at : at + 64] = jnp.concatenate([part(2 * j), part(2 * j + 1)], axis=1)

    pl.when(core_ref[0] == 0)(lambda: write((mine_ref, theirs_ref)))
    pl.when(core_ref[0] == 1)(lambda: write((theirs_ref, mine_ref)))


def planes_and_terms(core, scale, place, x, g, below, above, pair, other):
    vmem = pl.BlockSpec(memory_space=pltpu.VMEM)
    return pl.pallas_call(
        terms_kernel,
        in_specs=[pl.BlockSpec(memory_space=pltpu.SMEM)] * 2 + [vmem] * 7,
        out_specs=[vmem] * 4,
        out_shape=[pltpu.VMEM((640, 1024), BF)] * 2 + [jax.ShapeDtypeStruct((448, 128), F32)] * 2,
        scratch_shapes=[pltpu.VMEM((1280, 768), BF), pltpu.VMEM((576, 192), F32)]
        + [pltpu.VMEM((576, 1024), BF)] * 2,
        compiler_params=params(),
        cost_estimate=pl.CostEstimate(flops=10**10, bytes_accessed=10**7, transcendentals=0),
        name="terms",
    )(core, scale, place, x, g, below, above, pair, other)


def conv_kernel(half, planes_ref, weight_ref, after_ref, *refs):
    out_hbm, token_ref, even_ref, odd_ref, out_ref, sems = refs[-6:]
    row = iota((256, 128), 0)
    lane = row % 128
    y, x = lane // 10 - 1, lane % 10 - 1
    inner = (y >= 0) & (y < 8) & (x >= 0) & (x < 8)
    pick = jnp.where(
        inner & (iota((256, 128), 1) == (row // 128) * 64 + y * 8 + x), 1.0, 0.0
    ).astype(BF)

    def store(slot):
        return pltpu.make_async_copy(out_ref.at[slot], out_hbm.at[4 * half + slot], sems.at[slot])

    def multiply(slot, parts_ref):
        for zp in range(4):
            parts_ref[:, 256 * zp : 256 * zp + 256] = jnp.dot(
                weight_ref[...], taps(planes_ref, 4 * half + slot, 2 * zp, 2), preferred_element_type=F32
            )

    def add(slot, parts_ref):
        for zp in range(4):
            tiles = []
            for h in range(2):
                at = 256 * zp + 128 * h
                total = None
                for m, shift in enumerate(SHIFTS):
                    piece = parts_ref[64 * m : 64 * m + 64, at : at + 128]
                    if shift:
                        piece = pltpu.roll(piece, (-shift) % 128, 1)
                    total = piece if total is None else total + piece
                tiles.append(total.astype(BF))
            out_ref[slot, :, 128 * zp : 128 * zp + 128] = jnp.dot(
                jnp.concatenate(tiles, axis=1), pick, preferred_element_type=F32
            ).astype(BF)

    multiply(0, even_ref)
    for slot in range(4):
        now, later = (even_ref, odd_ref) if slot % 2 == 0 else (odd_ref, even_ref)
        if slot < 3:
            multiply(slot + 1, later)
        add(slot, now)
        store(slot).start()
    for slot in range(4):
        store(slot).wait()
    token_ref[...] = jnp.zeros_like(token_ref)


def conv(planes, weight, half, after, into=None):
    anywhere = pl.BlockSpec(memory_space=pl.ANY)
    vmem = pl.BlockSpec(memory_space=pltpu.VMEM)
    hbm = pl.BlockSpec(memory_space=pltpu.HBM)
    return pl.pallas_call(
        functools.partial(conv_kernel, half),
        in_specs=[vmem, vmem, anywhere] + [hbm] * (into is not None),
        out_specs=[hbm, vmem],
        out_shape=[
            jax.ShapeDtypeStruct((8, 64, 512), BF),
            jax.ShapeDtypeStruct((8, 128), F32),
        ],
        scratch_shapes=[pltpu.VMEM((576, 1024), F32)] * 2
        + [pltpu.VMEM((4, 64, 512), BF), pltpu.SemaphoreType.DMA((4,))],
        input_output_aliases={} if into is None else {3: 0},
        compiler_params=params(),
        cost_estimate=pl.CostEstimate(flops=3 * 10**9, bytes_accessed=10**6, transcendentals=0),
        name="conv",
    )(in_vmem(planes), in_vmem(weight), after, *([] if into is None else [into]))


def coords(i):
    t = i % 64
    return [i // 64, t // 16, (t // 8) % 2, (t // 2) % 4, t % 2]


AXIS = {"zl": (0, 4), "y": (1, 4), "zh": (2, 2), "x": (3, 4), "c": (4, 2)}


def shift_pairs(key, by):
    at, size = AXIS[key]
    out = []
    for i in range(N_DEV):
        v = coords(i)
        v[at] = (v[at] + by) % size
        out.append((i, v[0] * 64 + ((v[1] * 2 + v[2]) * 4 + v[3]) * 2 + v[4]))
    return out


def send(x, key, by):
    return lax.ppermute(x, AXES, shift_pairs(key, by))


def plus(terms, token=None):
    vmem = pl.BlockSpec(memory_space=pltpu.VMEM)
    tokens = [] if token is None else [token]

    def kernel(*refs):
        *parts, out_ref = refs[len(tokens) :]
        out_ref[...] = functools.reduce(jnp.add, [ref[...] for ref in parts])

    return pl.pallas_call(
        kernel,
        in_specs=[pl.BlockSpec(memory_space=pl.ANY)] * len(tokens) + [vmem] * len(terms),
        out_specs=vmem,
        out_shape=jax.ShapeDtypeStruct(terms[0].shape, F32),
        compiler_params=params(),
        name="plus",
    )(*tokens, *terms)


def cut_kernel(me_ref, mine_ref, got_ref, *refs):
    *out_refs, total_ref = refs
    total_ref[...] = mine_ref[...] + got_ref[...]
    for s, ref in enumerate(out_refs):
        at = lax.rem(me_ref[0] + s, 4) * 112
        ref[...] = total_ref[pl.ds(pl.multiple_of(at, 8), 112)]


def cut(me, mine, got):
    vmem = pl.BlockSpec(memory_space=pltpu.VMEM)
    return pl.pallas_call(
        cut_kernel,
        in_specs=[pl.BlockSpec(memory_space=pltpu.SMEM), vmem, vmem],
        out_specs=[vmem] * 4,
        out_shape=[jax.ShapeDtypeStruct((112, 128), F32)] * 4,
        scratch_shapes=[pltpu.VMEM((448, 128), F32)],
        compiler_params=params(),
        name="cut",
    )(me, mine, got)


def assemble_kernel(me_ref, token_ref, *refs):
    *parts, out_ref = refs
    rows = parts[0].shape[0]
    for s, ref in enumerate(parts):
        at = lax.rem(me_ref[0] + s, len(parts)) * rows
        out_ref[pl.ds(pl.multiple_of(at, 8), rows)] = ref[...]


def assemble(me, parts, token):
    vmem = pl.BlockSpec(memory_space=pltpu.VMEM)
    rows = parts[0].shape[0]
    return pl.pallas_call(
        assemble_kernel,
        in_specs=[pl.BlockSpec(memory_space=pltpu.SMEM), pl.BlockSpec(memory_space=pl.ANY)] + [vmem] * len(parts),
        out_specs=vmem,
        out_shape=jax.ShapeDtypeStruct((rows * len(parts), 128), F32),
        compiler_params=params(),
        name="assemble",
    )(me, token, *parts)


def finish_kernel(me_ref, mine_ref, other_ref, out_ref):
    def fill(parts):
        for j in range(14):
            wide = 64 if j == 13 else 128
            out_ref[:, 128 * j : 128 * j + wide] = parts[j // 7][64 * (j % 7) : 64 * (j % 7) + 64, :wide]

    pl.when(me_ref[0] == 0)(lambda: fill((mine_ref, other_ref)))
    pl.when(me_ref[0] == 1)(lambda: fill((other_ref, mine_ref)))


def finish(me, mine, other):
    vmem = pl.BlockSpec(memory_space=pltpu.VMEM)
    return pl.pallas_call(
        finish_kernel,
        in_specs=[pl.BlockSpec(memory_space=pltpu.SMEM), vmem, vmem],
        out_specs=vmem,
        out_shape=jax.ShapeDtypeStruct((64, 1728), F32),
        compiler_params=params(),
        name="finish",
    )(me, mine, other)


def shards(features, cotangent, weight, block_table):
    slab = lax.axis_index("slab")
    tile = lax.axis_index("tile")
    core = (tile % 2).astype(jnp.int32).reshape(1)
    table = jnp.pad(block_table, ((1, 1), (1, 1), (0, 0)), constant_values=-1)
    window = lax.dynamic_slice(table, (slab, tile * YR, 0), (3, 4, LX)).reshape(96)
    voxels = jnp.sum((block_table >= 0).astype(F32)) * 512.0
    scale = (1.0 / jnp.sqrt(voxels)).reshape(1)

    low, high, x_held, g_held = faces(features, cotangent)
    below = lax.ppermute(high, "slab", [(0, 1), (1, 2), (2, 3)])
    above = lax.ppermute(low, "slab", [(1, 0), (2, 1), (3, 2)])
    to_pair, to_other = edges(core, window, scale, x_held, g_held, below, above)
    pair = lax.ppermute(to_pair, "tile", [(i, i ^ 1) for i in range(64)])
    swaps = [(i, i + 1) for i in range(1, 63, 2)]
    other = lax.ppermute(to_other, "tile", swaps + [(b, a) for a, b in swaps])
    place, forward, backward = prepare(core, window, weight)

    x_planes, g_planes, mine, theirs = planes_and_terms(core, scale, place, x_held, g_held, below, above, pair, other)

    x = ((tile // 2) % 4).astype(jnp.int32).reshape(1)
    quarters = cut(x, mine, send(theirs, "c", 1))
    part = quarters[0]

    got = [send(quarters[s], "x", s) for s in (2, 3, 1)]
    conv_out, token = conv(x_planes, forward, 0, part)
    part = plus([part] + got, token)

    got = [send(part, "y", s) for s in (2, 3, 1)]
    conv_out, token = conv(x_planes, forward, 1, part, conv_out)
    part = plus([part] + got, token)

    got = [send(part, "zl", s) for s in (2, 3, 1)]
    grad_features, token = conv(g_planes, backward, 0, part)
    part = plus([part] + got, token)

    part = plus([part, send(part, "zh", 1)])

    got = [send(part, "x", -s) for s in (1, 2, 3)]
    grad_features, token = conv(g_planes, backward, 1, part, grad_features)
    half = assemble(x, [part] + got, token)

    grad_weight = finish(core, half, send(half, "c", 1))
    return conv_out, grad_features, grad_weight


def solution(mesh):
    rows = P(AXES, None, None)
    return jax.shard_map(
        shards,
        mesh=mesh,
        in_specs=(rows, rows, P(), P()),
        out_specs=(rows, rows, P()),
        check_vma=False,
    )
```

time: 115 us -> 85.7 us (0.75)
  local copies, waits for them, and re-layouts: 17.3 us -> 4.43 us
  Pallas kernels: 35.6 us -> 25.1 us
  waiting for transfers between devices: 17.8 us -> 7.43 us
  starting transfers between devices: 39.2 us -> 45.5 us
    ppermute x15, waiting for transfers between devices: 14.9 us -> 5.07 us  [send(): return lax.ppermute(x, AXES, shift_pairs(key, by))]
    pallas_call x4 -> x13, Pallas kernels: 25.6 us -> 17.9 us  [the longest x4 13.2 us: conv(): pl.pallas_call(functools.partial(conv_kernel, half), in_specs=[vmem, vmem...]
    ppermute x15, starting transfers between devices: 28.7 us -> 35.1 us  [send(): return lax.ppermute(x, AXES, shift_pairs(key, by))]
    unnamed x21 -> x8, local copies, waits for them, and re-layouts: 8.08 us -> 3.46 us
    transpose x3 -> x0, local copies, waits for them, and re-layouts: 4.34 us -> none  [the longest x2 3 us: shards(): backward = spread[:, ::-1, ::-1].transpose(2, 3, 1, 0).reshape(576, 192)]
    reshape x3 -> x0, local copies, waits for them, and re-layouts: 3.87 us -> none  [the longest x1 1.54 us: shards(): forward = spread.transpose(2, 0, 1, 3).reshape(576, 192)]
    pallas_call x1, Pallas kernels: 9.05 us -> 5.7 us  [planes_and_terms(): pl.pallas_call(terms_kernel, in_specs=[pl.BlockSpec(memory_space=pltpu.SM...]
  transfers between devices with their start and end apart: 19 -> 19, of which waited for: 10 -> 6; matrix products, arithmetic and copies ran while one was open for 9% -> 3% of each run, Pallas kernels for 22% -> 18%
where the time goes in v1:
time: 85.7 us; the launch traced here: 85.4 us
  starting transfers between devices  45.5 us (53%)
  Pallas kernels  25.1 us (29%)
  waiting for transfers between devices  7.43 us (9%)
  local copies, waits for them, and re-layouts  4.43 us (5%)
  between operations  1.57 us (2%)
  other arithmetic  1.33 us (2%)
    ppermute x15, starting transfers between devices, send(): return lax.ppermute(x, AXES, shift_pairs(key, by))  35.1 us
    pallas_call x4, Pallas kernels, conv(): pl.pallas_call(functools.partial(conv_kernel, half), in_specs=[vmem, vmem...  13.2 us
    pallas_call x1, Pallas kernels, planes_and_terms(): pl.pallas_call(terms_kernel, in_specs=[pl.BlockSpec(memory_space=pltpu.SM...  5.7 us
    ppermute x15, waiting for transfers between devices, send(): return lax.ppermute(x, AXES, shift_pairs(key, by))  5.07 us
    ppermute x1, starting transfers between devices, shards(): below = lax.ppermute(high, 'slab', [(0, 1), (1, 2), (2, 3)])  4.38 us
    unnamed x8, local copies, waits for them, and re-layouts  3.46 us
    ppermute x1, starting transfers between devices, shards(): other = lax.ppermute(to_other, 'tile', swaps + [(b, a) for a, b in swaps])  3.02 us
    pallas_call x1, Pallas kernels, prepare(): pl.pallas_call(prepare_kernel, in_specs=[smem, smem, pl.BlockSpec(memory_...  2.36 us
  transfers between devices with their start and end apart: 19, of which 6 were waited for; matrix products, arithmetic and copies ran while one was open for 3% of the time, Pallas kernels for 18%

profile of v1, /device:TPU:1, one launch (start us, length us, event | category | flops | bytes accessed | tf_op | source)
XLA Modules:
  0.0 85.4 jit_solution(925710205063397401)
XLA Ops:
  0.6 1.3 %faces.1 = (bf16[8,64,128]{2,1,0:T(8,128)(2,1)S(1)}, bf16[8,64,128]{2,1,0:T(8,128)(2,1)S(1)}, bf16[8,64,512]{2,1,0:T(8,128)(2,1)S(1)}, bf16[8,64,512]{2,1,0:T(8,128)(2,1)S(1)}) custom-call(bf16[8,64,512]{2,1,0:T(8,128)(2,1)} %x_ref.1, bf16[8,64,512]{2,1,0:T(8,128)(2,1)} %g_ref.1), custom_call_target="tpu_custom_call" | custom-call | tf_op jit(solution)/shard_map/faces/pallas_call | solution.py:62
  2.0 4.4 %collective-permute-start = (bf16[8,64,128]{2,1,0:T(8,128)(2,1)S(1)}, bf16[8,64,128]{2,1,0:T(8,128)(2,1)S(1)}, u32[]{:S(2)}, u32[]{:S(2)}) collective-permute-start(bf16[8,64,128]{2,1,0:T(8,128)(2,1)S(1)} %get-tuple-element.31), channel_id=1, source_target_pairs={{0,64},{64,128},{128,192},{1,65},{65,129},{129,193},{2,66},{66,130... | collective-permute-start | bytes 393224 | tf_op jit(solution)/shard_map/ppermute | solution.py:480
  6.3 1.3 %collective-permute-start.1 = (bf16[8,64,128]{2,1,0:T(8,128)(2,1)S(1)}, bf16[8,64,128]{2,1,0:T(8,128)(2,1)S(1)}, u32[]{:S(2)}, u32[]{:S(2)}) collective-permute-start(bf16[8,64,128]{2,1,0:T(8,128)(2,1)S(1)} %get-tuple-element.32), channel_id=1, source_target_pairs={{64,0},{128,64},{192,128},{65,1},{129,65},{193,129},{66,2},{130,66... | collective-permute-start | bytes 393224 | tf_op jit(solution)/shard_map/ppermute | solution.py:481
  7.6 1.3 %convert_reduce_fusion = f32[]{:T(128)} fusion(s32[4,128,8]{1,2,0:T(8,128)} %param.7), kind=kLoop, calls=%fused_computation.1 | loop fusion | flops 12287 | bytes 16388 | tf_op jit(solution)/shard_map/reduce_sum | solution.py:476
  10.7 2.0 %collective-permute-done.1.above_ref = bf16[8,64,128]{2,1,0:T(8,128)(2,1)S(1)} collective-permute-done((bf16[8,64,128]{2,1,0:T(8,128)(2,1)S(1)}, bf16[8,64,128]{2,1,0:T(8,128)(2,1)S(1)}, u32[]{:S(2)}, u32[]{:S(2)}) %collective-permute-start.1) | collective-permute-done | bytes 131104 | tf_op jit(solution)/shard_map/ppermute | solution.py:481
  12.7 1.5 %edges.1 = (bf16[320,128]{1,0:T(8,128)(2,1)S(1)}, bf16[320,128]{1,0:T(8,128)(2,1)S(1)}) custom-call(s32[1]{0:T(128)} %bitcast.core_ref.me_ref, s32[96]{0:T(128)S(1)} %reshape.20.table_ref.window_ref, f32[1]{0:T(128)} %bitcast.1.scale_ref, bf16[8,64,512]{2,1,0:T(8,128)(2,1)S(1)} %get-tuple-element.29.x_ref, bf16[8,64,512]{2,1,0:T(8,128)(2,1)S(1)} %get-tuple-element.30.g_ref, ...), custom_call_target="tpu_custom_call" | custom-call | tf_op jit(solution)/shard_map/edges/pallas_call | solution.py:111
  14.2 1.8 %collective-permute-start.2 = (bf16[320,128]{1,0:T(8,128)(2,1)S(1)}, bf16[320,128]{1,0:T(8,128)(2,1)S(1)}, u32[]{:S(2)}, u32[]{:S(2)}) collective-permute-start(bf16[320,128]{1,0:T(8,128)(2,1)S(1)} %get-tuple-element.33), channel_id=1, source_target_pairs={{0,1},{1,0},{2,3},{3,2},{4,5},{5,4},{6,7},{7,6},{8,9},{9,8},{10,11... | collective-permute-start | bytes 245768 | tf_op jit(solution)/shard_map/ppermute | solution.py:483
  16.0 3.0 %collective-permute-start.3 = (bf16[320,128]{1,0:T(8,128)(2,1)S(1)}, bf16[320,128]{1,0:T(8,128)(2,1)S(1)}, u32[]{:S(2)}, u32[]{:S(2)}) collective-permute-start(bf16[320,128]{1,0:T(8,128)(2,1)S(1)} %get-tuple-element.34), channel_id=1, source_target_pairs={{1,2},{3,4},{5,6},{7,8},{9,10},{11,12},{13,14},{15,16},{17,18},{19... | collective-permute-start | bytes 245768 | tf_op jit(solution)/shard_map/ppermute | solution.py:485
  19.0 2.4 %prepare.1 = (bf16[3,768,1024]{2,1,0:T(8,128)(2,1)S(1)}, bf16[576,192]{1,0:T(8,128)(2,1)S(1)}, bf16[576,192]{1,0:T(8,128)(2,1)S(1)}) custom-call(s32[1]{0:T(128)} %bitcast.core_ref.me_ref, s32[96]{0:T(128)S(1)} %reshape.20.table_ref.window_ref, bf16[64,1728]{1,0:T(8,128)(2,1)} %weight_hbm.1), custom_call_target="tpu_custom_call" | custom-call | tf_op jit(solution)/shard_map/prepare/pallas_call | solution.py:187
  21.7 5.7 %terms.1 = (bf16[640,1024]{1,0:T(8,128)(2,1)S(1)}, bf16[640,1024]{1,0:T(8,128)(2,1)S(1)}, f32[448,128]{1,0:T(8,128)S(1)}, f32[448,128]{1,0:T(8,128)S(1)}) custom-call(s32[1]{0:T(128)} %bitcast.core_ref.me_ref, f32[1]{0:T(128)} %bitcast.1.scale_ref, bf16[3,768,1024]{2,1,0:T(8,128)(2,1)S(1)} %get-tuple-element.28.place_ref, ...), custom_call_target="tpu_custom_call" | custom-call | flops 10000000000 | bytes 10000000 | tf_op jit(solution)/shard_map/terms/pallas_call | solution.py:285
  27.4 1.1 %copy-done = bf16[640,1024]{1,0:T(8,128)(2,1)} copy-done((bf16[640,1024]{1,0:T(8,128)(2,1)}, bf16[640,1024]{1,0:T(8,128)(2,1)S(1)}, u32[]{:S(2)}) %copy-start) | copy-done | bytes 1310744
  28.5 1.1 %copy-done.2 = bf16[640,1024]{1,0:T(8,128)(2,1)} copy-done((bf16[640,1024]{1,0:T(8,128)(2,1)}, bf16[640,1024]{1,0:T(8,128)(2,1)S(1)}, u32[]{:S(2)}) %copy-start.2) | copy-done | bytes 1310744
  29.6 1.5 %collective-permute-done.4.got_ref = f32[448,128]{1,0:T(8,128)S(1)} collective-permute-done((f32[448,128]{1,0:T(8,128)S(1)}, f32[448,128]{1,0:T(8,128)S(1)}, u32[]{:S(2)}, u32[]{:S(2)}) %collective-permute-start.4) | collective-permute-done | bytes 229408 | tf_op jit(solution)/shard_map/ppermute | solution.py:385
  31.1 2.9 %collective-permute-start.5 = (f32[112,128]{1,0:T(8,128)S(1)}, f32[112,128]{1,0:T(8,128)S(1)}, u32[]{:S(2)}, u32[]{:S(2)}) collective-permute-start(f32[112,128]{1,0:T(8,128)S(1)} %get-tuple-element.41), channel_id=1, source_target_pairs={{0,4},{1,5},{2,6},{3,7},{4,0},{5,1},{6,2},{7,3},{8,12},{9,13},{10,... | collective-permute-start | bytes 172040 | tf_op jit(solution)/shard_map/ppermute | solution.py:385
  34.0 5.8 %collective-permute-start.6 = (f32[112,128]{1,0:T(8,128)S(1)}, f32[112,128]{1,0:T(8,128)S(1)}, u32[]{:S(2)}, u32[]{:S(2)}) collective-permute-start(f32[112,128]{1,0:T(8,128)S(1)} %get-tuple-element.42), channel_id=1, source_target_pairs={{0,6},{1,7},{2,0},{3,1},{4,2},{5,3},{6,4},{7,5},{8,14},{9,15},{10,... | collective-permute-start | bytes 172040 | tf_op jit(solution)/shard_map/ppermute | solution.py:385
  40.3 1.3 %copy-done.3 = bf16[640,1024]{1,0:T(8,128)(2,1)S(1)} copy-done((bf16[640,1024]{1,0:T(8,128)(2,1)S(1)}, bf16[640,1024]{1,0:T(8,128)(2,1)}, u32[]{:S(2)}) %copy-start.3) | copy-done | bytes 1310744
  41.6 3.3 %conv.4 = (bf16[8,64,512]{2,1,0:T(8,128)(2,1)}, f32[8,128]{1,0:T(8,128)S(1)}) custom-call(bf16[640,1024]{1,0:T(8,128)(2,1)S(1)} %copy-done.3, bf16[576,192]{1,0:T(8,128)(2,1)S(1)} %get-tuple-element.36.weight_ref, f32[112,128]{1,0:T(8,128)S(1)} %get-tuple-element.39.after_ref.refs_1_), custom_call_target="tpu_custom_call" | custom-call | flops 3000000000 | bytes 1000000 | tf_op jit(solution)/shard_map/conv/pallas_call | solution.py:349
  45.0 1.4 %collective-permute-start.10 = (f32[112,128]{1,0:T(8,128)S(1)}, f32[112,128]{1,0:T(8,128)S(1)}, u32[]{:S(2)}, u32[]{:S(2)}) collective-permute-start(f32[112,128]{1,0:T(8,128)S(1)} %plus.4.after_ref.refs_1_), channel_id=1, source_target_pairs={{0,16},{1,17},{2,18},{3,19},{4,20},{5,21},{6,22},{7,23},{8,24},{9,... | collective-permute-start | bytes 172040 | tf_op jit(solution)/shard_map/ppermute | solution.py:385
  46.3 1.5 %collective-permute-start.9 = (f32[112,128]{1,0:T(8,128)S(1)}, f32[112,128]{1,0:T(8,128)S(1)}, u32[]{:S(2)}, u32[]{:S(2)}) collective-permute-start(f32[112,128]{1,0:T(8,128)S(1)} %plus.4.after_ref.refs_1_), channel_id=1, source_target_pairs={{0,48},{1,49},{2,50},{3,51},{4,52},{5,53},{6,54},{7,55},{8,56},{9,... | collective-permute-start | bytes 172040 | tf_op jit(solution)/shard_map/ppermute | solution.py:385
  47.9 1.6 %collective-permute-start.8 = (f32[112,128]{1,0:T(8,128)S(1)}, f32[112,128]{1,0:T(8,128)S(1)}, u32[]{:S(2)}, u32[]{:S(2)}) collective-permute-start(f32[112,128]{1,0:T(8,128)S(1)} %plus.4.after_ref.refs_1_), channel_id=1, source_target_pairs={{0,32},{1,33},{2,34},{3,35},{4,36},{5,37},{6,38},{7,39},{8,40},{9,... | collective-permute-start | bytes 172040 | tf_op jit(solution)/shard_map/ppermute | solution.py:385
  49.4 3.3 %conv.5 = (bf16[8,64,512]{2,1,0:T(8,128)(2,1)}, f32[8,128]{1,0:T(8,128)S(1)}) custom-call(bf16[640,1024]{1,0:T(8,128)(2,1)S(1)} %copy-done.3, bf16[576,192]{1,0:T(8,128)(2,1)S(1)} %get-tuple-element.36.weight_ref, f32[112,128]{1,0:T(8,128)S(1)} %plus.4.after_ref.refs_1_, bf16[8,64,512]{2,1,0:T(8,128)(2,1)} %get-tuple-element.44.refs_0_), custom_call_target="tpu_custom_call", output_to_operand_aliasing={{0}: (3, {})} | custom-call | flops 3000000000 | bytes 1000000 | tf_op jit(solution)/shard_map/conv/pallas_call | solution.py:349
  52.8 2.6 %collective-permute-start.13 = (f32[112,128]{1,0:T(8,128)S(1)}, f32[112,128]{1,0:T(8,128)S(1)}, u32[]{:S(2)}, u32[]{:S(2)}) collective-permute-start(f32[112,128]{1,0:T(8,128)S(1)} %plus.5.after_ref.refs_1_), channel_id=1, source_target_pairs={{0,64},{1,65},{2,66},{3,67},{4,68},{5,69},{6,70},{7,71},{8,72},{9,... | collective-permute-start | bytes 172040 | tf_op jit(solution)/shard_map/ppermute | solution.py:385
  56.1 1.3 %collective-permute-start.11 = (f32[112,128]{1,0:T(8,128)S(1)}, f32[112,128]{1,0:T(8,128)S(1)}, u32[]{:S(2)}, u32[]{:S(2)}) collective-permute-start(f32[112,128]{1,0:T(8,128)S(1)} %plus.5.after_ref.refs_1_), channel_id=1, source_target_pairs={{0,128},{1,129},{2,130},{3,131},{4,132},{5,133},{6,134},{7,135},{8... | collective-permute-start | bytes 172040 | tf_op jit(solution)/shard_map/ppermute | solution.py:385
  57.4 3.3 %conv.6 = (bf16[8,64,512]{2,1,0:T(8,128)(2,1)}, f32[8,128]{1,0:T(8,128)S(1)}) custom-call(bf16[640,1024]{1,0:T(8,128)(2,1)S(1)} %copy-done.1, bf16[576,192]{1,0:T(8,128)(2,1)S(1)} %get-tuple-element.47.weight_ref, f32[112,128]{1,0:T(8,128)S(1)} %plus.5.after_ref.refs_1_), custom_call_target="tpu_custom_call" | custom-call | flops 3000000000 | bytes 1000000 | tf_op jit(solution)/shard_map/conv/pallas_call | solution.py:349
  60.7 0.9 %collective-permute-done.11.refs_2_ = f32[112,128]{1,0:T(8,128)S(1)} collective-permute-done((f32[112,128]{1,0:T(8,128)S(1)}, f32[112,128]{1,0:T(8,128)S(1)}, u32[]{:S(2)}, u32[]{:S(2)}) %collective-permute-start.11) | collective-permute-done | bytes 57376 | tf_op jit(solution)/shard_map/ppermute | solution.py:385
  61.6 7.0 %collective-permute-start.14 = (f32[112,128]{1,0:T(8,128)S(1)}, f32[112,128]{1,0:T(8,128)S(1)}, u32[]{:S(2)}, u32[]{:S(2)}) collective-permute-start(f32[112,128]{1,0:T(8,128)S(1)} %plus.6.refs_0_), channel_id=1, source_target_pairs={{0,8},{1,9},{2,10},{3,11},{4,12},{5,13},{6,14},{7,15},{8,0},{9,1},... | collective-permute-start | bytes 172040 | tf_op jit(solution)/shard_map/ppermute | solution.py:385
  68.6 1.6 %collective-permute-done.14.refs_1_ = f32[112,128]{1,0:T(8,128)S(1)} collective-permute-done((f32[112,128]{1,0:T(8,128)S(1)}, f32[112,128]{1,0:T(8,128)S(1)}, u32[]{:S(2)}, u32[]{:S(2)}) %collective-permute-start.14) | collective-permute-done | bytes 57376 | tf_op jit(solution)/shard_map/ppermute | solution.py:385
  70.2 1.6 %collective-permute-start.17 = (f32[112,128]{1,0:T(8,128)S(1)}, f32[112,128]{1,0:T(8,128)S(1)}, u32[]{:S(2)}, u32[]{:S(2)}) collective-permute-start(f32[112,128]{1,0:T(8,128)S(1)} %plus.7.after_ref.refs_0_), channel_id=1, source_target_pairs={{0,2},{1,3},{2,4},{3,5},{4,6},{5,7},{6,0},{7,1},{8,10},{9,11},{10,... | collective-permute-start | bytes 172040 | tf_op jit(solution)/shard_map/ppermute | solution.py:385
  71.8 1.9 %collective-permute-start.16 = (f32[112,128]{1,0:T(8,128)S(1)}, f32[112,128]{1,0:T(8,128)S(1)}, u32[]{:S(2)}, u32[]{:S(2)}) collective-permute-start(f32[112,128]{1,0:T(8,128)S(1)} %plus.7.after_ref.refs_0_), channel_id=1, source_target_pairs={{0,4},{1,5},{2,6},{3,7},{4,0},{5,1},{6,2},{7,3},{8,12},{9,13},{10,... | collective-permute-start | bytes 172040 | tf_op jit(solution)/shard_map/ppermute | solution.py:385
  74.3 3.3 %conv.7 = (bf16[8,64,512]{2,1,0:T(8,128)(2,1)}, f32[8,128]{1,0:T(8,128)S(1)}) custom-call(bf16[640,1024]{1,0:T(8,128)(2,1)S(1)} %copy-done.1, bf16[576,192]{1,0:T(8,128)(2,1)S(1)} %get-tuple-element.47.weight_ref, f32[112,128]{1,0:T(8,128)S(1)} %plus.7.after_ref.refs_0_, bf16[8,64,512]{2,1,0:T(8,128)(2,1)} %get-tuple-element.50.refs_0_), custom_call_target="tpu_custom_call", output_to_operand_aliasing={{0}: (3, {})} | custom-call | flops 3000000000 | bytes 1000000 | tf_op jit(solution)/shard_map/conv/pallas_call | solution.py:349
  77.6 5.8 %collective-permute-start.18 = (f32[448,128]{1,0:T(8,128)S(1)}, f32[448,128]{1,0:T(8,128)S(1)}, u32[]{:S(2)}, u32[]{:S(2)}) collective-permute-start(f32[448,128]{1,0:T(8,128)S(1)} %assemble.1.mine_ref), channel_id=1, source_target_pairs={{0,1},{1,0},{2,3},{3,2},{4,5},{5,4},{6,7},{7,6},{8,9},{9,8},{10,11... | collective-permute-start | bytes 688136 | tf_op jit(solution)/shard_map/ppermute | solution.py:385
  83.4 1.1 %collective-permute-done.18.other_ref = f32[448,128]{1,0:T(8,128)S(1)} collective-permute-done((f32[448,128]{1,0:T(8,128)S(1)}, f32[448,128]{1,0:T(8,128)S(1)}, u32[]{:S(2)}, u32[]{:S(2)}) %collective-permute-start.18) | collective-permute-done | bytes 229408 | tf_op jit(solution)/shard_map/ppermute | solution.py:385
  (33 shorter events, 4.1 us)
Async XLA Ops:
  2.0 8.7 %collective-permute-start = (bf16[8,64,128]{2,1,0:T(8,128)(2,1)S(1)}, bf16[8,64,128]{2,1,0:T(8,128)(2,1)S(1)}, u32[]{:S(2)}, u32[]{:S(2)}) collective-permute-start(bf16[8,64,128]{2,1,0:T(8,128)(2,1)S(1)} %get-tuple-element.31), channel_id=1, source_target_pairs={{0,64},{64,128},{128,192},{1,65},{65,129},{129,193},{2,66},{66,130... | collective-permute-start | bytes 393224 | tf_op jit(solution)/shard_map/ppermute | solution.py:480
  6.3 6.3 %collective-permute-start.1 = (bf16[8,64,128]{2,1,0:T(8,128)(2,1)S(1)}, bf16[8,64,128]{2,1,0:T(8,128)(2,1)S(1)}, u32[]{:S(2)}, u32[]{:S(2)}) collective-permute-start(bf16[8,64,128]{2,1,0:T(8,128)(2,1)S(1)} %get-tuple-element.32), channel_id=1, source_target_pairs={{64,0},{128,64},{192,128},{65,1},{129,65},{193,129},{66,2},{130,66... | collective-permute-start | bytes 393224 | tf_op jit(solution)/shard_map/ppermute | solution.py:481
  14.2 7.1 %collective-permute-start.2 = (bf16[320,128]{1,0:T(8,128)(2,1)S(1)}, bf16[320,128]{1,0:T(8,128)(2,1)S(1)}, u32[]{:S(2)}, u32[]{:S(2)}) collective-permute-start(bf16[320,128]{1,0:T(8,128)(2,1)S(1)} %get-tuple-element.33), channel_id=1, source_target_pairs={{0,1},{1,0},{2,3},{3,2},{4,5},{5,4},{6,7},{7,6},{8,9},{9,8},{10,11... | collective-permute-start | bytes 245768 | tf_op jit(solution)/shard_map/ppermute | solution.py:483
  16.0 5.7 %collective-permute-start.3 = (bf16[320,128]{1,0:T(8,128)(2,1)S(1)}, bf16[320,128]{1,0:T(8,128)(2,1)S(1)}, u32[]{:S(2)}, u32[]{:S(2)}) collective-permute-start(bf16[320,128]{1,0:T(8,128)(2,1)S(1)} %get-tuple-element.34), channel_id=1, source_target_pairs={{1,2},{3,4},{5,6},{7,8},{9,10},{11,12},{13,14},{15,16},{17,18},{19... | collective-permute-start | bytes 245768 | tf_op jit(solution)/shard_map/ppermute | solution.py:485
  27.4 1.1 %copy-start = (bf16[640,1024]{1,0:T(8,128)(2,1)}, bf16[640,1024]{1,0:T(8,128)(2,1)S(1)}, u32[]{:S(2)}) copy-start(bf16[640,1024]{1,0:T(8,128)(2,1)S(1)} %get-tuple-element.46.planes_ref) | copy-start | bytes 3932164
  28.5 1.1 %copy-start.2 = (bf16[640,1024]{1,0:T(8,128)(2,1)}, bf16[640,1024]{1,0:T(8,128)(2,1)S(1)}, u32[]{:S(2)}) copy-start(bf16[640,1024]{1,0:T(8,128)(2,1)S(1)} %get-tuple-element.35.planes_ref) | copy-start | bytes 3932164
  29.6 1.5 %collective-permute-start.4 = (f32[448,128]{1,0:T(8,128)S(1)}, f32[448,128]{1,0:T(8,128)S(1)}, u32[]{:S(2)}, u32[]{:S(2)}) collective-permute-start(f32[448,128]{1,0:T(8,128)S(1)} %get-tuple-element.38), channel_id=1, source_target_pairs={{0,1},{1,0},{2,3},{3,2},{4,5},{5,4},{6,7},{7,6},{8,9},{9,8},{10,11... | collective-permute-start | bytes 688136 | tf_op jit(solution)/shard_map/ppermute | solution.py:385
  31.1 13.8 %collective-permute-start.5 = (f32[112,128]{1,0:T(8,128)S(1)}, f32[112,128]{1,0:T(8,128)S(1)}, u32[]{:S(2)}, u32[]{:S(2)}) collective-permute-start(f32[112,128]{1,0:T(8,128)S(1)} %get-tuple-element.41), channel_id=1, source_target_pairs={{0,4},{1,5},{2,6},{3,7},{4,0},{5,1},{6,2},{7,3},{8,12},{9,13},{10,... | collective-permute-start | bytes 172040 | tf_op jit(solution)/shard_map/ppermute | solution.py:385
  34.0 11.0 %collective-permute-start.6 = (f32[112,128]{1,0:T(8,128)S(1)}, f32[112,128]{1,0:T(8,128)S(1)}, u32[]{:S(2)}, u32[]{:S(2)}) collective-permute-start(f32[112,128]{1,0:T(8,128)S(1)} %get-tuple-element.42), channel_id=1, source_target_pairs={{0,6},{1,7},{2,0},{3,1},{4,2},{5,3},{6,4},{7,5},{8,14},{9,15},{10,... | collective-permute-start | bytes 172040 | tf_op jit(solution)/shard_map/ppermute | solution.py:385
  39.8 5.2 %collective-permute-start.7 = (f32[112,128]{1,0:T(8,128)S(1)}, f32[112,128]{1,0:T(8,128)S(1)}, u32[]{:S(2)}, u32[]{:S(2)}) collective-permute-start(f32[112,128]{1,0:T(8,128)S(1)} %get-tuple-element.43), channel_id=1, source_target_pairs={{0,2},{1,3},{2,4},{3,5},{4,6},{5,7},{6,0},{7,1},{8,10},{9,11},{10,... | collective-permute-start | bytes 172040 | tf_op jit(solution)/shard_map/ppermute | solution.py:385
  40.3 1.3 %copy-start.3 = (bf16[640,1024]{1,0:T(8,128)(2,1)S(1)}, bf16[640,1024]{1,0:T(8,128)(2,1)}, u32[]{:S(2)}) copy-start(bf16[640,1024]{1,0:T(8,128)(2,1)} %copy-done.2) | copy-start | bytes 3932164
  45.0 7.8 %collective-permute-start.10 = (f32[112,128]{1,0:T(8,128)S(1)}, f32[112,128]{1,0:T(8,128)S(1)}, u32[]{:S(2)}, u32[]{:S(2)}) collective-permute-start(f32[112,128]{1,0:T(8,128)S(1)} %plus.4.after_ref.refs_1_), channel_id=1, source_target_pairs={{0,16},{1,17},{2,18},{3,19},{4,20},{5,21},{6,22},{7,23},{8,24},{9,... | collective-permute-start | bytes 172040 | tf_op jit(solution)/shard_map/ppermute | solution.py:385
  46.3 6.4 %collective-permute-start.9 = (f32[112,128]{1,0:T(8,128)S(1)}, f32[112,128]{1,0:T(8,128)S(1)}, u32[]{:S(2)}, u32[]{:S(2)}) collective-permute-start(f32[112,128]{1,0:T(8,128)S(1)} %plus.4.after_ref.refs_1_), channel_id=1, source_target_pairs={{0,48},{1,49},{2,50},{3,51},{4,52},{5,53},{6,54},{7,55},{8,56},{9,... | collective-permute-start | bytes 172040 | tf_op jit(solution)/shard_map/ppermute | solution.py:385
  47.9 4.9 %collective-permute-start.8 = (f32[112,128]{1,0:T(8,128)S(1)}, f32[112,128]{1,0:T(8,128)S(1)}, u32[]{:S(2)}, u32[]{:S(2)}) collective-permute-start(f32[112,128]{1,0:T(8,128)S(1)} %plus.4.after_ref.refs_1_), channel_id=1, source_target_pairs={{0,32},{1,33},{2,34},{3,35},{4,36},{5,37},{6,38},{7,39},{8,40},{9,... | collective-permute-start | bytes 172040 | tf_op jit(solution)/shard_map/ppermute | solution.py:385
  49.4 8.0 %copy-start.1 = (bf16[640,1024]{1,0:T(8,128)(2,1)S(1)}, bf16[640,1024]{1,0:T(8,128)(2,1)}, u32[]{:S(2)}) copy-start(bf16[640,1024]{1,0:T(8,128)(2,1)} %copy-done) | copy-start | bytes 3932164
  52.8 7.9 %collective-permute-start.13 = (f32[112,128]{1,0:T(8,128)S(1)}, f32[112,128]{1,0:T(8,128)S(1)}, u32[]{:S(2)}, u32[]{:S(2)}) collective-permute-start(f32[112,128]{1,0:T(8,128)S(1)} %plus.5.after_ref.refs_1_), channel_id=1, source_target_pairs={{0,64},{1,65},{2,66},{3,67},{4,68},{5,69},{6,70},{7,71},{8,72},{9,... | collective-permute-start | bytes 172040 | tf_op jit(solution)/shard_map/ppermute | solution.py:385
  55.4 5.4 %collective-permute-start.12 = (f32[112,128]{1,0:T(8,128)S(1)}, f32[112,128]{1,0:T(8,128)S(1)}, u32[]{:S(2)}, u32[]{:S(2)}) collective-permute-start(f32[112,128]{1,0:T(8,128)S(1)} %plus.5.after_ref.refs_1_), channel_id=1, source_target_pairs={{0,192},{1,193},{2,194},{3,195},{4,196},{5,197},{6,198},{7,199},{8... | collective-permute-start | bytes 172040 | tf_op jit(solution)/shard_map/ppermute | solution.py:385
  56.1 5.5 %collective-permute-start.11 = (f32[112,128]{1,0:T(8,128)S(1)}, f32[112,128]{1,0:T(8,128)S(1)}, u32[]{:S(2)}, u32[]{:S(2)}) collective-permute-start(f32[112,128]{1,0:T(8,128)S(1)} %plus.5.after_ref.refs_1_), channel_id=1, source_target_pairs={{0,128},{1,129},{2,130},{3,131},{4,132},{5,133},{6,134},{7,135},{8... | collective-permute-start | bytes 172040 | tf_op jit(solution)/shard_map/ppermute | solution.py:385
  61.6 8.6 %collective-permute-start.14 = (f32[112,128]{1,0:T(8,128)S(1)}, f32[112,128]{1,0:T(8,128)S(1)}, u32[]{:S(2)}, u32[]{:S(2)}) collective-permute-start(f32[112,128]{1,0:T(8,128)S(1)} %plus.6.refs_0_), channel_id=1, source_target_pairs={{0,8},{1,9},{2,10},{3,11},{4,12},{5,13},{6,14},{7,15},{8,0},{9,1},... | collective-permute-start | bytes 172040 | tf_op jit(solution)/shard_map/ppermute | solution.py:385
  70.2 7.4 %collective-permute-start.17 = (f32[112,128]{1,0:T(8,128)S(1)}, f32[112,128]{1,0:T(8,128)S(1)}, u32[]{:S(2)}, u32[]{:S(2)}) collective-permute-start(f32[112,128]{1,0:T(8,128)S(1)} %plus.7.after_ref.refs_0_), channel_id=1, source_target_pairs={{0,2},{1,3},{2,4},{3,5},{4,6},{5,7},{6,0},{7,1},{8,10},{9,11},{10,... | collective-permute-start | bytes 172040 | tf_op jit(solution)/shard_map/ppermute | solution.py:385
  71.8 5.8 %collective-permute-start.16 = (f32[112,128]{1,0:T(8,128)S(1)}, f32[112,128]{1,0:T(8,128)S(1)}, u32[]{:S(2)}, u32[]{:S(2)}) collective-permute-start(f32[112,128]{1,0:T(8,128)S(1)} %plus.7.after_ref.refs_0_), channel_id=1, source_target_pairs={{0,4},{1,5},{2,6},{3,7},{4,0},{5,1},{6,2},{7,3},{8,12},{9,13},{10,... | collective-permute-start | bytes 172040 | tf_op jit(solution)/shard_map/ppermute | solution.py:385
  73.7 3.9 %collective-permute-start.15 = (f32[112,128]{1,0:T(8,128)S(1)}, f32[112,128]{1,0:T(8,128)S(1)}, u32[]{:S(2)}, u32[]{:S(2)}) collective-permute-start(f32[112,128]{1,0:T(8,128)S(1)} %plus.7.after_ref.refs_0_), channel_id=1, source_target_pairs={{0,6},{1,7},{2,0},{3,1},{4,2},{5,3},{6,4},{7,5},{8,14},{9,15},{10,... | collective-permute-start | bytes 172040 | tf_op jit(solution)/shard_map/ppermute | solution.py:385
  77.6 6.9 %collective-permute-start.18 = (f32[448,128]{1,0:T(8,128)S(1)}, f32[448,128]{1,0:T(8,128)S(1)}, u32[]{:S(2)}, u32[]{:S(2)}) collective-permute-start(f32[448,128]{1,0:T(8,128)S(1)} %assemble.1.mine_ref), channel_id=1, source_target_pairs={{0,1},{1,0},{2,3},{3,2},{4,5},{5,4},{6,7},{7,6},{8,9},{9,8},{10,11... | collective-permute-start | bytes 688136 | tf_op jit(solution)/shard_map/ppermute | solution.py:385

commit v2 on v1

--- a/solution.py
+++ b/solution.py
@@ -13,12 +13,12 @@
 F32 = jnp.float32
 AXES = ("slab", "tile")
 N_DEV = 256
-VMEM_LIMIT = 24 * 1024 * 1024
+MIB = 1024 * 1024
 SHIFTS = [dy * 10 + dx for dy in (-1, 0, 1) for dx in (-1, 0, 1)]
 
 
-def params():
-    return pltpu.CompilerParams(vmem_limit_bytes=VMEM_LIMIT)
+def params(mib=6):
+    return pltpu.CompilerParams(vmem_limit_bytes=mib * MIB)
 
 
 def iota(shape, dim):
@@ -38,7 +38,7 @@
     return pltpu.with_memory_space_constraint(x, pltpu.VMEM)
 
 
-def faces_kernel(x_ref, g_ref, low_ref, high_ref, xv_ref, gv_ref, sems):
+def edges_kernel(core_ref, x_ref, g_ref, pair_ref, other_ref, xv_ref, gv_ref, sems):
     copies = [
         pltpu.make_async_copy(src.at[4 * h : 4 * h + 4], dst.at[4 * h : 4 * h + 4], sems.at[2 * h + i])
         for h in range(2)
@@ -46,82 +46,86 @@
     ]
     for copy in copies:
         copy.start()
-    for h in range(2):
+    chunk = iota((1024, 128), 0) // 128
+    lane = iota((1024, 128), 0) % 128
+    at = (lane // 64) * 64 + chunk * 8 + lane % 8
+    match = at == iota((1024, 128), 1)
+    found = []
+    for h, y in ((0, 0), (1, 7)):
+        edge = jnp.where(match & ((lane // 8) % 8 == y), 1.0, 0.0).astype(BF)
         for copy in copies[2 * h : 2 * h + 2]:
             copy.wait()
-        for s in range(4 * h, 4 * h + 4):
-            low_ref[s] = halves(xv_ref[s, :, :128], gv_ref[s, :, :128], False)
-            high_ref[s] = halves(xv_ref[s, :, 384:], gv_ref[s, :, 384:], True)
-
-
-def faces(x, g):
-    vmem = pl.BlockSpec(memory_space=pltpu.VMEM)
-    hbm = pl.BlockSpec(memory_space=pltpu.HBM)
-    face = jax.ShapeDtypeStruct((8, 64, 128), BF)
-    held = pltpu.VMEM((8, 64, 512), BF)
-    return pl.pallas_call(
-        faces_kernel,
-        in_specs=[hbm, hbm],
-        out_specs=[vmem] * 4,
-        out_shape=[face, face, held, held],
-        scratch_shapes=[pltpu.SemaphoreType.DMA((4,))],
-        compiler_params=params(),
-        name="faces",
-    )(in_hbm(x), in_hbm(g))
-
-
-def edges_kernel(core_ref, window_ref, scale_ref, x_ref, g_ref, below_ref, above_ref, pair_ref, other_ref):
-    chunk = iota((1024, 128), 0) // 128
-    lane = iota((1024, 128), 0) % 128
-    to = iota((1024, 128), 1)
-
-    def picks(y):
-        here = (lane // 8) % 8 == y
-        edge = (lane // 64) * 64 + chunk * 8 + lane % 8
-        line = (chunk // 4) * 64 + (lane // 64) * 32 + (chunk % 4) * 8 + lane % 8
-        return [
-            jnp.where(here & (at == to), 1.0, 0.0).astype(BF) for at in (edge, line)
-        ]
-
-    found = []
-    for first, y in ((4, 7), (0, 0)):
-        edge, line = picks(y)
         rows = [
             jnp.concatenate(
-                [ref[first + s, :, 128 * t : 128 * t + 128] for ref in (x_ref, g_ref) for s in range(4)],
+                [ref[4 * h + s, :, 128 * t : 128 * t + 128] for ref in (xv_ref, gv_ref) for s in range(4)],
                 axis=1,
             )
             for t in range(4)
         ]
-        lines = jnp.concatenate(
-            [ref[first + s] for ref in (below_ref, above_ref) for s in range(4)], axis=1
-        )
-        main = jnp.dot(jnp.concatenate(rows, axis=0), edge, preferred_element_type=F32)
-        last = jnp.dot(lines, line, preferred_element_type=F32)
-        found.append(jnp.concatenate([main, last], axis=0))
-    up, down = found
+        found.append(jnp.dot(jnp.concatenate(rows, axis=0), edge, preferred_element_type=F32))
+    down, up = found
     odd = core_ref[0]
     pair_ref[...] = jnp.where(odd == 0, up, down).astype(BF)
     other_ref[...] = jnp.where(odd == 0, down, up).astype(BF)
 
 
-def edges(core, window, scale, x, g, below, above):
-    out = jax.ShapeDtypeStruct((320, 128), BF)
-    vmem = pl.BlockSpec(memory_space=pltpu.VMEM)
+def edges(core, x, g):
+    vmem = pl.BlockSpec(memory_space=pltpu.VMEM)
+    hbm = pl.BlockSpec(memory_space=pltpu.HBM)
+    edge = jax.ShapeDtypeStruct((256, 128), BF)
+    held = pltpu.VMEM((8, 64, 512), BF)
     return pl.pallas_call(
         edges_kernel,
-        in_specs=[pl.BlockSpec(memory_space=pltpu.SMEM)] * 3 + [vmem] * 4,
+        in_specs=[pl.BlockSpec(memory_space=pltpu.SMEM), hbm, hbm],
+        out_specs=[vmem] * 4,
+        out_shape=[edge, edge, held, held],
+        scratch_shapes=[pltpu.SemaphoreType.DMA((4,))],
+        compiler_params=params(12),
+        name="edges",
+    )(core, in_hbm(x), in_hbm(g))
+
+
+def faces_kernel(x_ref, g_ref, low_ref, high_ref):
+    for s in range(8):
+        low_ref[s] = halves(x_ref[s, :, :128], g_ref[s, :, :128], False)
+        high_ref[s] = halves(x_ref[s, :, 384:], g_ref[s, :, 384:], True)
+
+
+def faces(x, g):
+    vmem = pl.BlockSpec(memory_space=pltpu.VMEM)
+    return pl.pallas_call(
+        faces_kernel,
+        in_specs=[vmem, vmem],
         out_specs=[vmem, vmem],
-        out_shape=[out, out],
+        out_shape=[jax.ShapeDtypeStruct((8, 64, 128), BF)] * 2,
+        compiler_params=params(8),
+        name="faces",
+    )(in_vmem(x), in_vmem(g))
+
+
+def lines_kernel(pair_ref, other_ref, low_ref, high_ref):
+    low_ref[...] = halves(pair_ref[:64], other_ref[:64], False)
+    high_ref[...] = halves(pair_ref[192:], other_ref[192:], True)
+
+
+def lines(pair, other):
+    vmem = pl.BlockSpec(memory_space=pltpu.VMEM)
+    return pl.pallas_call(
+        lines_kernel,
+        in_specs=[vmem, vmem],
+        out_specs=[vmem, vmem],
+        out_shape=[jax.ShapeDtypeStruct((64, 128), BF)] * 2,
         compiler_params=params(),
-        name="edges",
-    )(core, window, scale, x, g, below, above)
-
-
-def prepare_kernel(core_ref, table_ref, weight_hbm, place_ref, forward_ref, backward_ref, weight_ref, sem):
+        name="lines",
+    )(pair, other)
+
+
+def weights_kernel(after_ref, blocks_ref, weight_hbm, forward_ref, backward_ref, scale_ref, weight_ref, sem):
     load = pltpu.make_async_copy(weight_hbm, weight_ref, sem)
     load.start()
-    fill_places(core_ref, table_ref, place_ref)
+    active = jnp.sum(jnp.where(blocks_ref[...] >= 0, 1.0, 0.0), axis=0)
+    voxels = jnp.sum(jnp.sum(active, axis=1, keepdims=True), axis=0, keepdims=True) * 512.0
+    scale_ref[...] = jnp.broadcast_to(1.0 / jnp.sqrt(voxels), (8, 128))
     load.wait()
     rows = iota((128, 128), 0)
     same = jnp.where(rows == iota((128, 128), 1), 1.0, 0.0).astype(BF)
@@ -139,6 +143,20 @@
         for k in range(2 * j, 2 * j + wide // 64):
             dz, m = (26 - k) // 9, (26 - k) % 9
             backward_ref[64 * m : 64 * m + 64, 64 * dz : 64 * dz + 64] = turned[64 * (k - 2 * j) : 64 * (k - 2 * j) + 64]
+
+
+def arranged_weights(weight, blocks, after):
+    vmem = pl.BlockSpec(memory_space=pltpu.VMEM)
+    turned = pltpu.VMEM((576, 192), BF)
+    return pl.pallas_call(
+        weights_kernel,
+        in_specs=[pl.BlockSpec(memory_space=pl.ANY), vmem, pl.BlockSpec(memory_space=pltpu.HBM)],
+        out_specs=[vmem] * 3,
+        out_shape=[turned, turned, jax.ShapeDtypeStruct((8, 128), F32)],
+        scratch_shapes=[pltpu.VMEM((64, 1728), BF), pltpu.SemaphoreType.DMA],
+        compiler_params=params(),
+        name="weights",
+    )(after, blocks, in_hbm(weight))
 
 
 def fill_places(core_ref, table_ref, place_ref):
@@ -180,27 +198,23 @@
             ).astype(BF)
 
 
-def prepare(core, window, weight):
+def places(core, window):
     smem = pl.BlockSpec(memory_space=pltpu.SMEM)
-    vmem = pl.BlockSpec(memory_space=pltpu.VMEM)
-    turned = pltpu.VMEM((576, 192), BF)
-    return pl.pallas_call(
-        prepare_kernel,
-        in_specs=[smem, smem, pl.BlockSpec(memory_space=pltpu.HBM)],
-        out_specs=[vmem] * 3,
-        out_shape=[pltpu.VMEM((3, 768, 1024), BF), turned, turned],
-        scratch_shapes=[pltpu.VMEM((64, 1728), BF), pltpu.SemaphoreType.DMA],
-        compiler_params=params(),
-        name="prepare",
-    )(core, window, in_hbm(weight))
-
-
-def taps(planes_ref, slot, z_from, z_count):
-    at = slice(128 * slot, 128 * slot + 128)
+    return pl.pallas_call(
+        fill_places,
+        in_specs=[smem, smem],
+        out_specs=pl.BlockSpec(memory_space=pltpu.VMEM),
+        out_shape=pltpu.VMEM((3, 768, 1024), BF),
+        compiler_params=params(12),
+        name="places",
+    )(core, window)
+
+
+def taps(planes_ref, z_from, z_count):
     return jnp.concatenate(
         [
             jnp.concatenate(
-                [planes_ref[64 * (z + dz) : 64 * (z + dz) + 64, at] for z in range(z_from, z_from + z_count)],
+                [planes_ref[64 * (z + dz) : 64 * (z + dz) + 64] for z in range(z_from, z_from + z_count)],
                 axis=1,
             )
             for dz in range(3)
@@ -209,12 +223,11 @@
     )
 
 
-def terms_kernel(core_ref, scale_ref, place_ref, x_ref, g_ref, below_ref, above_ref, pair_ref, other_ref, x_planes_ref, g_planes_ref, mine_ref, theirs_ref, left_ref, total_ref, even_ref, odd_ref):
-    def fill(row, tiles, right, band, lane_group):
+def terms_kernel(core_ref, place_ref, x_ref, g_ref, below_ref, above_ref, below_line_ref, above_line_ref, pair_ref, other_ref, xa_ref, xb_hbm, ga_hbm, gb_hbm, mine_ref, theirs_ref, left_ref, total_ref, even_ref, odd_ref, xb_ref, ga_ref, gb_ref, sems):
+    def fill(row, tiles, right, sides):
         for j in range(4):
             left_ref[row : row + 64, 128 * j : 128 * j + 128] = halves(tiles[2 * j], tiles[2 * j + 1], right)
-        for side, ref in enumerate((pair_ref, other_ref)):
-            tile = ref[64 * band : 64 * band + 64]
+        for side, (tile, lane_group) in enumerate(sides):
             if lane_group:
                 tile = pltpu.roll(tile, 128 - 32 * lane_group, 1)
             left_ref[row : row + 64, 512 + 128 * side : 640 + 128 * side] = tile
@@ -222,26 +235,40 @@
     for a, ref in enumerate((x_ref, g_ref)):
         for t in range(4):
             tiles = [ref[s, :, 128 * t : 128 * t + 128] for s in range(8)]
+            band = [edge[64 * t : 64 * t + 64] for edge in (pair_ref, other_ref)]
             for parity in range(2):
-                fill(512 * a + 64 * (2 * t + parity), tiles, parity, t, 2 * parity + a)
-    for side, ref in enumerate((below_ref, above_ref)):
+                fill(512 * a + 64 * (2 * t + parity), tiles, parity, [(tile, 2 * parity + a) for tile in band])
+    for side, (ref, line_ref) in enumerate(((below_ref, below_line_ref), (above_ref, above_line_ref))):
         tiles = [ref[s] for s in range(8)]
+        line = line_ref[...]
         for a in range(2):
-            fill(1024 + 128 * side + 64 * a, tiles, a, 4, 2 * side + a)
-
-    for a, ref in enumerate((x_planes_ref, g_planes_ref)):
-        ref[64:576] = jnp.dot(
+            fill(1024 + 128 * side + 64 * a, tiles, a, [(line, a), (line, 2 + a)])
+
+    x_planes = [(xa_ref, xb_ref)[slot // 4].at[slot % 4] for slot in range(8)]
+    g_planes = [(ga_ref, gb_ref)[slot // 4].at[slot % 4] for slot in range(8)]
+    for a, planes in enumerate((x_planes, g_planes)):
+        main = jnp.dot(
             left_ref[512 * a : 512 * a + 512], place_ref[1], preferred_element_type=F32
         ).astype(BF)
+        for slot in range(8):
+            planes[slot][64:576] = main[:, 128 * slot : 128 * slot + 128]
     for side in range(2):
         both = jnp.dot(
             left_ref[1024 + 128 * side : 1152 + 128 * side],
             place_ref[2 * side],
             preferred_element_type=F32,
         ).astype(BF)
-        x_planes_ref[576 * side : 576 * side + 64] = both[:64]
-        g_planes_ref[576 * side : 576 * side + 64] = both[64:]
-
+        for slot in range(8):
+            at = slice(128 * slot, 128 * slot + 128)
+            x_planes[slot][576 * side : 576 * side + 64] = both[:64, at]
+            g_planes[slot][576 * side : 576 * side + 64] = both[64:, at]
+
+    stores = [
+        pltpu.make_async_copy(src, dst, sems.at[i])
+        for i, (src, dst) in enumerate(((xb_ref, xb_hbm), (ga_ref, ga_hbm), (gb_ref, gb_hbm)))
+    ]
+    for store in stores:
+        store.start()
     total_ref[...] = jnp.zeros_like(total_ref)
     lane = iota((64, 128), 1)
     column = lane % 10
@@ -249,8 +276,7 @@
 
     def move(slot, moved_ref):
         for z in range(8):
-            at = slice(128 * slot, 128 * slot + 128)
-            own = jnp.where(inner, g_planes_ref[64 * (z + 1) : 64 * (z + 1) + 64, at], jnp.zeros((), BF))
+            own = jnp.where(inner, g_planes[slot][64 * (z + 1) : 64 * (z + 1) + 64], jnp.zeros((), BF))
             for m, shift in enumerate(SHIFTS):
                 moved_ref[64 * m : 64 * m + 64, 128 * z : 128 * z + 128] = (
                     pltpu.roll(own, shift % 128, 1) if shift else own
@@ -262,14 +288,13 @@
         if slot < 7:
             move(slot + 1, later)
         total_ref[...] += lax.dot_general(
-            now[...], taps(x_planes_ref, slot, 0, 8), (((1,), (1,)), ((), ())), preferred_element_type=F32
+            now[...], taps(x_planes[slot], 0, 8), (((1,), (1,)), ((), ())), preferred_element_type=F32
         )
-    scale = scale_ref[0]
 
     def part(k):
         if k == 27:
             return jnp.zeros((64, 64), F32)
-        return total_ref[64 * (k % 9) : 64 * (k % 9) + 64, 64 * (k // 9) : 64 * (k // 9) + 64] * scale
+        return total_ref[64 * (k % 9) : 64 * (k % 9) + 64, 64 * (k // 9) : 64 * (k // 9) + 64]
 
     def write(refs):
         for j in range(14):
@@ -278,21 +303,25 @@
 
     pl.when(core_ref[0] == 0)(lambda: write((mine_ref, theirs_ref)))
     pl.when(core_ref[0] == 1)(lambda: write((theirs_ref, mine_ref)))
-
-
-def planes_and_terms(core, scale, place, x, g, below, above, pair, other):
+    for store in stores:
+        store.wait()
+
+
+def planes_and_terms(core, place, x, g, *halo):
     vmem = pl.BlockSpec(memory_space=pltpu.VMEM)
     return pl.pallas_call(
         terms_kernel,
-        in_specs=[pl.BlockSpec(memory_space=pltpu.SMEM)] * 2 + [vmem] * 7,
-        out_specs=[vmem] * 4,
-        out_shape=[pltpu.VMEM((640, 1024), BF)] * 2 + [jax.ShapeDtypeStruct((448, 128), F32)] * 2,
+        in_specs=[pl.BlockSpec(memory_space=pltpu.SMEM)] + [vmem] * 9,
+        out_specs=[vmem] + [pl.BlockSpec(memory_space=pltpu.HBM)] * 3 + [vmem] * 2,
+        out_shape=[pltpu.VMEM((4, 640, 128), BF)] + [pltpu.HBM((4, 640, 128), BF)] * 3 + [jax.ShapeDtypeStruct((448, 128), F32)] * 2,
         scratch_shapes=[pltpu.VMEM((1280, 768), BF), pltpu.VMEM((576, 192), F32)]
-        + [pltpu.VMEM((576, 1024), BF)] * 2,
-        compiler_params=params(),
+        + [pltpu.VMEM((576, 1024), BF)] * 2
+        + [pltpu.VMEM((4, 640, 128), BF)] * 3
+        + [pltpu.SemaphoreType.DMA((3,))],
+        compiler_params=params(24),
         cost_estimate=pl.CostEstimate(flops=10**10, bytes_accessed=10**7, transcendentals=0),
         name="terms",
-    )(core, scale, place, x, g, below, above, pair, other)
+    )(core, place, x, g, *halo)
 
 
 def conv_kernel(half, planes_ref, weight_ref, after_ref, *refs):
@@ -311,7 +340,7 @@
     def multiply(slot, parts_ref):
         for zp in range(4):
             parts_ref[:, 256 * zp : 256 * zp + 256] = jnp.dot(
-                weight_ref[...], taps(planes_ref, 4 * half + slot, 2 * zp, 2), preferred_element_type=F32
+                weight_ref[...], taps(planes_ref.at[slot], 2 * zp, 2), preferred_element_type=F32
             )
 
     def add(slot, parts_ref):
@@ -357,7 +386,7 @@
         scratch_shapes=[pltpu.VMEM((576, 1024), F32)] * 2
         + [pltpu.VMEM((4, 64, 512), BF), pltpu.SemaphoreType.DMA((4,))],
         input_output_aliases={} if into is None else {3: 0},
-        compiler_params=params(),
+        compiler_params=params(16),
         cost_estimate=pl.CostEstimate(flops=3 * 10**9, bytes_accessed=10**6, transcendentals=0),
         name="conv",
     )(in_vmem(planes), in_vmem(weight), after, *([] if into is None else [into]))
@@ -445,26 +474,28 @@
     )(me, token, *parts)
 
 
-def finish_kernel(me_ref, mine_ref, other_ref, out_ref):
+def finish_kernel(me_ref, scale_ref, mine_ref, other_ref, out_ref):
     def fill(parts):
         for j in range(14):
             wide = 64 if j == 13 else 128
-            out_ref[:, 128 * j : 128 * j + wide] = parts[j // 7][64 * (j % 7) : 64 * (j % 7) + 64, :wide]
+            out_ref[:, 128 * j : 128 * j + wide] = (
+                parts[j // 7][64 * (j % 7) : 64 * (j % 7) + 64, :wide] * scale_ref[0:1, :wide]
+            )
 
     pl.when(me_ref[0] == 0)(lambda: fill((mine_ref, other_ref)))
     pl.when(me_ref[0] == 1)(lambda: fill((other_ref, mine_ref)))
 
 
-def finish(me, mine, other):
+def finish(me, scale, mine, other):
     vmem = pl.BlockSpec(memory_space=pltpu.VMEM)
     return pl.pallas_call(
         finish_kernel,
-        in_specs=[pl.BlockSpec(memory_space=pltpu.SMEM), vmem, vmem],
+        in_specs=[pl.BlockSpec(memory_space=pltpu.SMEM)] + [vmem] * 3,
         out_specs=vmem,
         out_shape=jax.ShapeDtypeStruct((64, 1728), F32),
         compiler_params=params(),
         name="finish",
-    )(me, mine, other)
+    )(me, scale, mine, other)
 
 
 def shards(features, cotangent, weight, block_table):
@@ -473,43 +504,48 @@
     core = (tile % 2).astype(jnp.int32).reshape(1)
     table = jnp.pad(block_table, ((1, 1), (1, 1), (0, 0)), constant_values=-1)
     window = lax.dynamic_slice(table, (slab, tile * YR, 0), (3, 4, LX)).reshape(96)
-    voxels = jnp.sum((block_table >= 0).astype(F32)) * 512.0
-    scale = (1.0 / jnp.sqrt(voxels)).reshape(1)
-
-    low, high, x_held, g_held = faces(features, cotangent)
-    below = lax.ppermute(high, "slab", [(0, 1), (1, 2), (2, 3)])
-    above = lax.ppermute(low, "slab", [(1, 0), (2, 1), (3, 2)])
-    to_pair, to_other = edges(core, window, scale, x_held, g_held, below, above)
-    pair = lax.ppermute(to_pair, "tile", [(i, i ^ 1) for i in range(64)])
+    to_pair, to_other, x_held, g_held = edges(core, features, cotangent)
     swaps = [(i, i + 1) for i in range(1, 63, 2)]
     other = lax.ppermute(to_other, "tile", swaps + [(b, a) for a, b in swaps])
-    place, forward, backward = prepare(core, window, weight)
-
-    x_planes, g_planes, mine, theirs = planes_and_terms(core, scale, place, x_held, g_held, below, above, pair, other)
+    pair = lax.ppermute(to_pair, "tile", [(i, i ^ 1) for i in range(64)])
+    rise, fall = [(0, 1), (1, 2), (2, 3)], [(1, 0), (2, 1), (3, 2)]
+    low, high = faces(x_held, g_held)
+    below = lax.ppermute(high, "slab", rise)
+    above = lax.ppermute(low, "slab", fall)
+    low_line, high_line = lines(pair, other)
+    below_line = lax.ppermute(high_line, "slab", rise)
+    above_line = lax.ppermute(low_line, "slab", fall)
+    place = places(core, window)
+
+    xa, xb, ga, gb, mine, theirs = planes_and_terms(
+        core, place, x_held, g_held, below, above, below_line, above_line, pair, other
+    )
 
     x = ((tile // 2) % 4).astype(jnp.int32).reshape(1)
     quarters = cut(x, mine, send(theirs, "c", 1))
     part = quarters[0]
 
     got = [send(quarters[s], "x", s) for s in (2, 3, 1)]
-    conv_out, token = conv(x_planes, forward, 0, part)
+    forward, backward, scale = arranged_weights(weight, block_table, part)
+    part = plus([part] + got, scale)
+
+    got = [send(part, "y", s) for s in (2, 3, 1)]
+    conv_out, token = conv(xa, forward, 0, part)
     part = plus([part] + got, token)
 
-    got = [send(part, "y", s) for s in (2, 3, 1)]
-    conv_out, token = conv(x_planes, forward, 1, part, conv_out)
+    got = [send(part, "zl", s) for s in (2, 3, 1)]
+    conv_out, token = conv(xb, forward, 1, part, conv_out)
     part = plus([part] + got, token)
 
-    got = [send(part, "zl", s) for s in (2, 3, 1)]
-    grad_features, token = conv(g_planes, backward, 0, part)
-    part = plus([part] + got, token)
-
-    part = plus([part, send(part, "zh", 1)])
+    got = send(part, "zh", 1)
+    grad_features, token = conv(ga, backward, 0, part)
+    part = plus([part, got], token)
 
     got = [send(part, "x", -s) for s in (1, 2, 3)]
-    grad_features, token = conv(g_planes, backward, 1, part, grad_features)
+    grad_features, token = conv(gb, backward, 1, part, grad_features)
     half = assemble(x, [part] + got, token)
 
-    grad_weight = finish(core, half, send(half, "c", 1))
+    grad_weight = finish(core, scale, half, send(half, "c", 1))
     return conv_out, grad_features, grad_weight
 
 

time: 85.7 us -> 82.3 us (0.960)
  local copies, waits for them, and re-layouts: 4.43 us -> 1.11 us
  waiting for transfers between devices: 7.43 us -> 9.91 us
  other arithmetic: 1.33 us -> 0 us
    ppermute x15, starting transfers between devices: 35.1 us -> 30.3 us  [send(): return lax.ppermute(x, AXES, shift_pairs(key, by))]
    ppermute x15, waiting for transfers between devices: 5.07 us -> 9.48 us  [send(): return lax.ppermute(x, AXES, shift_pairs(key, by))]
    ppermute x2 -> x4, starting transfers between devices: 5.67 us -> 9.67 us  [the longest x1 4.16 us: shards(): below_line = lax.ppermute(high_line, 'slab', rise)]
    unnamed x8 -> x9, local copies, waits for them, and re-layouts: 3.46 us -> 0.14 us
    ppermute x2 -> x4, waiting for transfers between devices: 2.01 us -> 0.42 us  [the longest x1 0.41 us: shards(): above_line = lax.ppermute(low_line, 'slab', fall)]
    ppermute x1, starting transfers between devices: 1.75 us -> 3.33 us  [shards(): pair = lax.ppermute(to_pair, 'tile', [(i, i ^ 1) for i in range(64)])]
    reduce_sum x1 -> x0, other arithmetic: 1.33 us -> none  [shards(): voxels = jnp.sum((block_table >= 0).astype(F32)) * 512.0]
    ppermute x1, starting transfers between devices: 3.02 us -> 1.91 us  [shards(): other = lax.ppermute(to_other, 'tile', swaps + [(b, a) for a, b in swaps])]
  transfers between devices with their start and end apart: 19 -> 21, of which waited for: 6 -> 10; matrix products, arithmetic and copies ran while one was open for 3% -> 1% of each run, Pallas kernels for 18% -> 20%
where the time goes in v2:
time: 82.3 us; the launch traced here: 82 us
  starting transfers between devices  45.2 us (55%)
  Pallas kernels  24.9 us (30%)
  waiting for transfers between devices  9.91 us (12%)
  local copies, waits for them, and re-layouts  1.11 us (1%)
  between operations  0.92 us (1%)
    ppermute x15, starting transfers between devices, send(): return lax.ppermute(x, AXES, shift_pairs(key, by))  30.3 us
    pallas_call x4, Pallas kernels, conv(): pl.pallas_call(functools.partial(conv_kernel, half), in_specs=[vmem, vmem...  13.2 us
    ppermute x15, waiting for transfers between devices, send(): return lax.ppermute(x, AXES, shift_pairs(key, by))  9.48 us
    pallas_call x1, Pallas kernels, planes_and_terms(): pl.pallas_call(terms_kernel, in_specs=[pl.BlockSpec(memory_space=pltpu.SM...  5.66 us
    ppermute x1, starting transfers between devices, shards(): below_line = lax.ppermute(high_line, 'slab', rise)  4.16 us
    ppermute x1, starting transfers between devices, shards(): pair = lax.ppermute(to_pair, 'tile', [(i, i ^ 1) for i in range(64)])  3.33 us
    ppermute x1, starting transfers between devices, shards(): below = lax.ppermute(high, 'slab', rise)  2.92 us
    pallas_call x1, Pallas kernels, places(): pl.pallas_call(fill_places, in_specs=[smem, smem], out_specs=pl.BlockSpec...  1.95 us
  transfers between devices with their start and end apart: 21, of which 10 were waited for; matrix products, arithmetic and copies ran while one was open for 1% of the time, Pallas kernels for 20%

profile of v2, /device:TPU:1, one launch (start us, length us, event | category | flops | bytes accessed | tf_op | source)
XLA Modules:
  0.0 82.0 jit_solution(733416588596330910)
XLA Ops:
  0.6 1.6 %edges.1 = (bf16[256,128]{1,0:T(8,128)(2,1)S(1)}, bf16[256,128]{1,0:T(8,128)(2,1)S(1)}, bf16[8,64,512]{2,1,0:T(8,128)(2,1)S(1)}, bf16[8,64,512]{2,1,0:T(8,128)(2,1)S(1)}) custom-call(s32[1]{0:T(128)} %bitcast.core_ref.me_ref, bf16[8,64,512]{2,1,0:T(8,128)(2,1)} %x_ref.1, bf16[8,64,512]{2,1,0:T(8,128)(2,1)} %g_ref.1), custom_call_target="tpu_custom_call" | custom-call | tf_op jit(solution)/shard_map/edges/pallas_call | solution.py:77
  2.3 3.3 %collective-permute-start.2 = (bf16[256,128]{1,0:T(8,128)(2,1)S(1)}, bf16[256,128]{1,0:T(8,128)(2,1)S(1)}, u32[]{:S(2)}, u32[]{:S(2)}) collective-permute-start(bf16[256,128]{1,0:T(8,128)(2,1)S(1)} %get-tuple-element.36), channel_id=1, source_target_pairs={{0,1},{1,0},{2,3},{3,2},{4,5},{5,4},{6,7},{7,6},{8,9},{9,8},{10,11... | collective-permute-start | bytes 196616 | tf_op jit(solution)/shard_map/ppermute | solution.py:510
  5.6 1.9 %collective-permute-start.3 = (bf16[256,128]{1,0:T(8,128)(2,1)S(1)}, bf16[256,128]{1,0:T(8,128)(2,1)S(1)}, u32[]{:S(2)}, u32[]{:S(2)}) collective-permute-start(bf16[256,128]{1,0:T(8,128)(2,1)S(1)} %get-tuple-element.37), channel_id=1, source_target_pairs={{1,2},{3,4},{5,6},{7,8},{9,10},{11,12},{13,14},{15,16},{17,18},{19... | collective-permute-start | bytes 196616 | tf_op jit(solution)/shard_map/ppermute | solution.py:509
  7.7 2.9 %collective-permute-start = (bf16[8,64,128]{2,1,0:T(8,128)(2,1)S(1)}, bf16[8,64,128]{2,1,0:T(8,128)(2,1)S(1)}, u32[]{:S(2)}, u32[]{:S(2)}) collective-permute-start(bf16[8,64,128]{2,1,0:T(8,128)(2,1)S(1)} %get-tuple-element.34), channel_id=1, source_target_pairs={{0,64},{64,128},{128,192},{1,65},{65,129},{129,193},{2,66},{66,130... | collective-permute-start | bytes 393224 | tf_op jit(solution)/shard_map/ppermute | solution.py:513
  10.6 1.3 %collective-permute-start.1 = (bf16[8,64,128]{2,1,0:T(8,128)(2,1)S(1)}, bf16[8,64,128]{2,1,0:T(8,128)(2,1)S(1)}, u32[]{:S(2)}, u32[]{:S(2)}) collective-permute-start(bf16[8,64,128]{2,1,0:T(8,128)(2,1)S(1)} %get-tuple-element.35), channel_id=1, source_target_pairs={{64,0},{128,64},{192,128},{65,1},{129,65},{193,129},{66,2},{130,66... | collective-permute-start | bytes 393224 | tf_op jit(solution)/shard_map/ppermute | solution.py:514
  12.0 4.2 %collective-permute-start.4 = (bf16[64,128]{1,0:T(8,128)(2,1)S(1)}, bf16[64,128]{1,0:T(8,128)(2,1)S(1)}, u32[]{:S(2)}, u32[]{:S(2)}) collective-permute-start(bf16[64,128]{1,0:T(8,128)(2,1)S(1)} %get-tuple-element.38), channel_id=1, source_target_pairs={{0,64},{64,128},{128,192},{1,65},{65,129},{129,193},{2,66},{66,130... | collective-permute-start | bytes 49160 | tf_op jit(solution)/shard_map/ppermute | solution.py:516
  16.2 1.3 %collective-permute-start.5 = (bf16[64,128]{1,0:T(8,128)(2,1)S(1)}, bf16[64,128]{1,0:T(8,128)(2,1)S(1)}, u32[]{:S(2)}, u32[]{:S(2)}) collective-permute-start(bf16[64,128]{1,0:T(8,128)(2,1)S(1)} %get-tuple-element.39), channel_id=1, source_target_pairs={{64,0},{128,64},{192,128},{65,1},{129,65},{193,129},{66,2},{130,66... | collective-permute-start | bytes 49160 | tf_op jit(solution)/shard_map/ppermute | solution.py:517
  17.5 0.8 pad_dynamic-slice_fusion
  18.5 1.9 %places.1.place_ref = bf16[3,768,1024]{2,1,0:T(8,128)(2,1)S(1)} custom-call(s32[1]{0:T(128)} %bitcast.core_ref.me_ref, s32[96]{0:T(128)S(1)} %reshape.16.table_ref), custom_call_target="tpu_custom_call" | custom-call | tf_op jit(solution)/shard_map/places/pallas_call | solution.py:203
  20.9 5.7 %terms.1 = (bf16[4,640,128]{2,1,0:T(8,128)(2,1)S(1)}, bf16[4,640,128]{2,1,0:T(8,128)(2,1)}, bf16[4,640,128]{2,1,0:T(8,128)(2,1)}, bf16[4,640,128]{2,1,0:T(8,128)...) custom-call(s32[1]{0:T(128)} %bitcast.core_ref.me_ref, bf16[3,768,1024]{2,1,0:T(8,128)(2,1)S(1)} %places.1.place_ref, ...), custom_call_target="tpu_custom_call" | custom-call | flops 10000000000 | bytes 10000000 | tf_op jit(solution)/shard_map/terms/pallas_call | solution.py:312
  26.7 1.4 %collective-permute-done.6.got_ref = f32[448,128]{1,0:T(8,128)S(1)} collective-permute-done((f32[448,128]{1,0:T(8,128)S(1)}, f32[448,128]{1,0:T(8,128)S(1)}, u32[]{:S(2)}, u32[]{:S(2)}) %collective-permute-start.6) | collective-permute-done | bytes 229408 | tf_op jit(solution)/shard_map/ppermute | solution.py:414
  28.1 3.6 %collective-permute-start.7 = (f32[112,128]{1,0:T(8,128)S(1)}, f32[112,128]{1,0:T(8,128)S(1)}, u32[]{:S(2)}, u32[]{:S(2)}) collective-permute-start(f32[112,128]{1,0:T(8,128)S(1)} %get-tuple-element.47), channel_id=1, source_target_pairs={{0,4},{1,5},{2,6},{3,7},{4,0},{5,1},{6,2},{7,3},{8,12},{9,13},{10,... | collective-permute-start | bytes 172040 | tf_op jit(solution)/shard_map/ppermute | solution.py:414
  31.8 3.4 %collective-permute-start.8 = (f32[112,128]{1,0:T(8,128)S(1)}, f32[112,128]{1,0:T(8,128)S(1)}, u32[]{:S(2)}, u32[]{:S(2)}) collective-permute-start(f32[112,128]{1,0:T(8,128)S(1)} %get-tuple-element.48), channel_id=1, source_target_pairs={{0,6},{1,7},{2,0},{3,1},{4,2},{5,3},{6,4},{7,5},{8,14},{9,15},{10,... | collective-permute-start | bytes 172040 | tf_op jit(solution)/shard_map/ppermute | solution.py:414
  35.8 1.3 %weights.1 = (bf16[576,192]{1,0:T(8,128)(2,1)S(1)}, bf16[576,192]{1,0:T(8,128)(2,1)S(1)}, f32[8,128]{1,0:T(8,128)S(1)}) custom-call(f32[112,128]{1,0:T(8,128)S(1)} %get-tuple-element.43.after_ref.refs_1_, s32[4,128,8]{2,1,0:T(8,128)S(1)} %copy.10.blocks_ref, bf16[64,1728]{1,0:T(8,128)(2,1)} %weight_hbm.1), custom_call_target="tpu_custom_call" | custom-call | tf_op jit(solution)/shard_map/weights/pallas_call | solution.py:151
  37.2 1.6 %collective-permute-done.8.refs_3_ = f32[112,128]{1,0:T(8,128)S(1)} collective-permute-done((f32[112,128]{1,0:T(8,128)S(1)}, f32[112,128]{1,0:T(8,128)S(1)}, u32[]{:S(2)}, u32[]{:S(2)}) %collective-permute-start.8) | collective-permute-done | bytes 57376 | tf_op jit(solution)/shard_map/ppermute | solution.py:414
  39.4 6.8 %collective-permute-start.10 = (f32[112,128]{1,0:T(8,128)S(1)}, f32[112,128]{1,0:T(8,128)S(1)}, u32[]{:S(2)}, u32[]{:S(2)}) collective-permute-start(f32[112,128]{1,0:T(8,128)S(1)} %plus.4.after_ref.refs_1_), channel_id=1, source_target_pairs={{0,32},{1,33},{2,34},{3,35},{4,36},{5,37},{6,38},{7,39},{8,40},{9,... | collective-permute-start | bytes 172040 | tf_op jit(solution)/shard_map/ppermute | solution.py:414
  46.3 0.8 collective-permute-start.11
  47.0 0.7 collective-permute-start.12
  47.7 3.3 %conv.4 = (bf16[8,64,512]{2,1,0:T(8,128)(2,1)}, f32[8,128]{1,0:T(8,128)S(1)}) custom-call(bf16[4,640,128]{2,1,0:T(8,128)(2,1)S(1)} %get-tuple-element.45.planes_ref, bf16[576,192]{1,0:T(8,128)(2,1)S(1)} %get-tuple-element.44.weight_ref, f32[112,128]{1,0:T(8,128)S(1)} %plus.4.after_ref.refs_1_), custom_call_target="tpu_custom_call" | custom-call | flops 3000000000 | bytes 1000000 | tf_op jit(solution)/shard_map/conv/pallas_call | solution.py:378
  51.3 1.6 %collective-permute-start.13 = (f32[112,128]{1,0:T(8,128)S(1)}, f32[112,128]{1,0:T(8,128)S(1)}, u32[]{:S(2)}, u32[]{:S(2)}) collective-permute-start(f32[112,128]{1,0:T(8,128)S(1)} %plus.5.after_ref.refs_1_), channel_id=1, source_target_pairs={{0,128},{1,129},{2,130},{3,131},{4,132},{5,133},{6,134},{7,135},{8... | collective-permute-start | bytes 172040 | tf_op jit(solution)/shard_map/ppermute | solution.py:414
  52.9 1.6 %collective-permute-start.14 = (f32[112,128]{1,0:T(8,128)S(1)}, f32[112,128]{1,0:T(8,128)S(1)}, u32[]{:S(2)}, u32[]{:S(2)}) collective-permute-start(f32[112,128]{1,0:T(8,128)S(1)} %plus.5.after_ref.refs_1_), channel_id=1, source_target_pairs={{0,192},{1,193},{2,194},{3,195},{4,196},{5,197},{6,198},{7,199},{8... | collective-permute-start | bytes 172040 | tf_op jit(solution)/shard_map/ppermute | solution.py:414
  54.5 3.3 %conv.5 = (bf16[8,64,512]{2,1,0:T(8,128)(2,1)}, f32[8,128]{1,0:T(8,128)S(1)}) custom-call(bf16[4,640,128]{2,1,0:T(8,128)(2,1)S(1)} %copy-done.1, bf16[576,192]{1,0:T(8,128)(2,1)S(1)} %get-tuple-element.44.weight_ref, f32[112,128]{1,0:T(8,128)S(1)} %plus.5.after_ref.refs_1_, ...), custom_call_target="tpu_custom_call", output_to_operand_aliasing={{0}: (3, {})} | custom-call | flops 3000000000 | bytes 1000000 | tf_op jit(solution)/shard_map/conv/pallas_call | solution.py:378
  57.8 2.0 %collective-permute-done.15.refs_4_ = f32[112,128]{1,0:T(8,128)S(1)} collective-permute-done((f32[112,128]{1,0:T(8,128)S(1)}, f32[112,128]{1,0:T(8,128)S(1)}, u32[]{:S(2)}, u32[]{:S(2)}) %collective-permute-start.15) | collective-permute-done | bytes 57376 | tf_op jit(solution)/shard_map/ppermute | solution.py:414
  59.9 2.2 %collective-permute-start.16 = (f32[112,128]{1,0:T(8,128)S(1)}, f32[112,128]{1,0:T(8,128)S(1)}, u32[]{:S(2)}, u32[]{:S(2)}) collective-permute-start(f32[112,128]{1,0:T(8,128)S(1)} %plus.6.after_ref.refs_1_), channel_id=1, source_target_pairs={{0,8},{1,9},{2,10},{3,11},{4,12},{5,13},{6,14},{7,15},{8,0},{9,1},... | collective-permute-start | bytes 172040 | tf_op jit(solution)/shard_map/ppermute | solution.py:414
  62.1 3.3 %conv.6 = (bf16[8,64,512]{2,1,0:T(8,128)(2,1)}, f32[8,128]{1,0:T(8,128)S(1)}) custom-call(bf16[4,640,128]{2,1,0:T(8,128)(2,1)S(1)} %copy-done.2, bf16[576,192]{1,0:T(8,128)(2,1)S(1)} %get-tuple-element.54.weight_ref, f32[112,128]{1,0:T(8,128)S(1)} %plus.6.after_ref.refs_1_), custom_call_target="tpu_custom_call" | custom-call | flops 3000000000 | bytes 1000000 | tf_op jit(solution)/shard_map/conv/pallas_call | solution.py:378
  65.4 1.5 %collective-permute-done.16.refs_2_ = f32[112,128]{1,0:T(8,128)S(1)} collective-permute-done((f32[112,128]{1,0:T(8,128)S(1)}, f32[112,128]{1,0:T(8,128)S(1)}, u32[]{:S(2)}, u32[]{:S(2)}) %collective-permute-start.16) | collective-permute-done | bytes 57376 | tf_op jit(solution)/shard_map/ppermute | solution.py:414
  66.9 0.8 collective-permute-start.17
  67.7 0.9 %collective-permute-start.19 = (f32[112,128]{1,0:T(8,128)S(1)}, f32[112,128]{1,0:T(8,128)S(1)}, u32[]{:S(2)}, u32[]{:S(2)}) collective-permute-start(f32[112,128]{1,0:T(8,128)S(1)} %plus.7.after_ref.refs_0_), channel_id=1, source_target_pairs={{0,2},{1,3},{2,4},{3,5},{4,6},{5,7},{6,0},{7,1},{8,10},{9,11},{10,... | collective-permute-start | bytes 172040 | tf_op jit(solution)/shard_map/ppermute | solution.py:414
  68.6 3.3 %conv.7 = (bf16[8,64,512]{2,1,0:T(8,128)(2,1)}, f32[8,128]{1,0:T(8,128)S(1)}) custom-call(bf16[4,640,128]{2,1,0:T(8,128)(2,1)S(1)} %copy-done, bf16[576,192]{1,0:T(8,128)(2,1)S(1)} %get-tuple-element.54.weight_ref, f32[112,128]{1,0:T(8,128)S(1)} %plus.7.after_ref.refs_0_, bf16[8,64,512]{2,1,0:T(8,128)(2,1)} %get-tuple-element.58.refs_0_), custom_call_target="tpu_custom_call", output_to_operand_aliasing={{0}: (3, {})} | custom-call | flops 3000000000 | bytes 1000000 | tf_op jit(solution)/shard_map/conv/pallas_call | solution.py:378
  72.9 7.3 %collective-permute-start.20 = (f32[448,128]{1,0:T(8,128)S(1)}, f32[448,128]{1,0:T(8,128)S(1)}, u32[]{:S(2)}, u32[]{:S(2)}) collective-permute-start(f32[448,128]{1,0:T(8,128)S(1)} %assemble.1.mine_ref), channel_id=1, source_target_pairs={{0,1},{1,0},{2,3},{3,2},{4,5},{5,4},{6,7},{7,6},{8,9},{9,8},{10,11... | collective-permute-start | bytes 688136 | tf_op jit(solution)/shard_map/ppermute | solution.py:414
  80.1 1.1 %collective-permute-done.20.other_ref = f32[448,128]{1,0:T(8,128)S(1)} collective-permute-done((f32[448,128]{1,0:T(8,128)S(1)}, f32[448,128]{1,0:T(8,128)S(1)}, u32[]{:S(2)}, u32[]{:S(2)}) %collective-permute-start.20) | collective-permute-done | bytes 229408 | tf_op jit(solution)/shard_map/ppermute | solution.py:414
  81.2 0.8 finish.1
  (39 shorter events, 3.5 us)
Async XLA Ops:
  2.3 9.6 %collective-permute-start.2 = (bf16[256,128]{1,0:T(8,128)(2,1)S(1)}, bf16[256,128]{1,0:T(8,128)(2,1)S(1)}, u32[]{:S(2)}, u32[]{:S(2)}) collective-permute-start(bf16[256,128]{1,0:T(8,128)(2,1)S(1)} %get-tuple-element.36), channel_id=1, source_target_pairs={{0,1},{1,0},{2,3},{3,2},{4,5},{5,4},{6,7},{7,6},{8,9},{9,8},{10,11... | collective-permute-start | bytes 196616 | tf_op jit(solution)/shard_map/ppermute | solution.py:510
  5.6 6.3 %collective-permute-start.3 = (bf16[256,128]{1,0:T(8,128)(2,1)S(1)}, bf16[256,128]{1,0:T(8,128)(2,1)S(1)}, u32[]{:S(2)}, u32[]{:S(2)}) collective-permute-start(bf16[256,128]{1,0:T(8,128)(2,1)S(1)} %get-tuple-element.37), channel_id=1, source_target_pairs={{1,2},{3,4},{5,6},{7,8},{9,10},{11,12},{13,14},{15,16},{17,18},{19... | collective-permute-start | bytes 196616 | tf_op jit(solution)/shard_map/ppermute | solution.py:509
  7.7 13.2 %collective-permute-start = (bf16[8,64,128]{2,1,0:T(8,128)(2,1)S(1)}, bf16[8,64,128]{2,1,0:T(8,128)(2,1)S(1)}, u32[]{:S(2)}, u32[]{:S(2)}) collective-permute-start(bf16[8,64,128]{2,1,0:T(8,128)(2,1)S(1)} %get-tuple-element.34), channel_id=1, source_target_pairs={{0,64},{64,128},{128,192},{1,65},{65,129},{129,193},{2,66},{66,130... | collective-permute-start | bytes 393224 | tf_op jit(solution)/shard_map/ppermute | solution.py:513
  10.6 10.2 %collective-permute-start.1 = (bf16[8,64,128]{2,1,0:T(8,128)(2,1)S(1)}, bf16[8,64,128]{2,1,0:T(8,128)(2,1)S(1)}, u32[]{:S(2)}, u32[]{:S(2)}) collective-permute-start(bf16[8,64,128]{2,1,0:T(8,128)(2,1)S(1)} %get-tuple-element.35), channel_id=1, source_target_pairs={{64,0},{128,64},{192,128},{65,1},{129,65},{193,129},{66,2},{130,66... | collective-permute-start | bytes 393224 | tf_op jit(solution)/shard_map/ppermute | solution.py:514
  12.0 8.4 %collective-permute-start.4 = (bf16[64,128]{1,0:T(8,128)(2,1)S(1)}, bf16[64,128]{1,0:T(8,128)(2,1)S(1)}, u32[]{:S(2)}, u32[]{:S(2)}) collective-permute-start(bf16[64,128]{1,0:T(8,128)(2,1)S(1)} %get-tuple-element.38), channel_id=1, source_target_pairs={{0,64},{64,128},{128,192},{1,65},{65,129},{129,193},{2,66},{66,130... | collective-permute-start | bytes 49160 | tf_op jit(solution)/shard_map/ppermute | solution.py:516
  16.2 4.7 %collective-permute-start.5 = (bf16[64,128]{1,0:T(8,128)(2,1)S(1)}, bf16[64,128]{1,0:T(8,128)(2,1)S(1)}, u32[]{:S(2)}, u32[]{:S(2)}) collective-permute-start(bf16[64,128]{1,0:T(8,128)(2,1)S(1)} %get-tuple-element.39), channel_id=1, source_target_pairs={{64,0},{128,64},{192,128},{65,1},{129,65},{193,129},{66,2},{130,66... | collective-permute-start | bytes 49160 | tf_op jit(solution)/shard_map/ppermute | solution.py:517
  20.4 15.3 %copy-start.3 = (s32[4,128,8]{1,2,0:T(8,128)S(1)}, s32[4,128,8]{1,2,0:T(8,128)}, u32[]{:S(2)}) copy-start(s32[4,128,8]{1,2,0:T(8,128)} %param.7) | copy-start | bytes 49156
  26.5 1.6 %collective-permute-start.6 = (f32[448,128]{1,0:T(8,128)S(1)}, f32[448,128]{1,0:T(8,128)S(1)}, u32[]{:S(2)}, u32[]{:S(2)}) collective-permute-start(f32[448,128]{1,0:T(8,128)S(1)} %get-tuple-element.42), channel_id=1, source_target_pairs={{0,1},{1,0},{2,3},{3,2},{4,5},{5,4},{6,7},{7,6},{8,9},{9,8},{10,11... | collective-permute-start | bytes 688136 | tf_op jit(solution)/shard_map/ppermute | solution.py:414
  28.1 9.0 %collective-permute-start.7 = (f32[112,128]{1,0:T(8,128)S(1)}, f32[112,128]{1,0:T(8,128)S(1)}, u32[]{:S(2)}, u32[]{:S(2)}) collective-permute-start(f32[112,128]{1,0:T(8,128)S(1)} %get-tuple-element.47), channel_id=1, source_target_pairs={{0,4},{1,5},{2,6},{3,7},{4,0},{5,1},{6,2},{7,3},{8,12},{9,13},{10,... | collective-permute-start | bytes 172040 | tf_op jit(solution)/shard_map/ppermute | solution.py:414
  31.8 7.1 %collective-permute-start.8 = (f32[112,128]{1,0:T(8,128)S(1)}, f32[112,128]{1,0:T(8,128)S(1)}, u32[]{:S(2)}, u32[]{:S(2)}) collective-permute-start(f32[112,128]{1,0:T(8,128)S(1)} %get-tuple-element.48), channel_id=1, source_target_pairs={{0,6},{1,7},{2,0},{3,1},{4,2},{5,3},{6,4},{7,5},{8,14},{9,15},{10,... | collective-permute-start | bytes 172040 | tf_op jit(solution)/shard_map/ppermute | solution.py:414
  35.2 4.2 %collective-permute-start.9 = (f32[112,128]{1,0:T(8,128)S(1)}, f32[112,128]{1,0:T(8,128)S(1)}, u32[]{:S(2)}, u32[]{:S(2)}) collective-permute-start(f32[112,128]{1,0:T(8,128)S(1)} %get-tuple-element.49), channel_id=1, source_target_pairs={{0,2},{1,3},{2,4},{3,5},{4,6},{5,7},{6,0},{7,1},{8,10},{9,11},{10,... | collective-permute-start | bytes 172040 | tf_op jit(solution)/shard_map/ppermute | solution.py:414
  39.4 11.6 %collective-permute-start.10 = (f32[112,128]{1,0:T(8,128)S(1)}, f32[112,128]{1,0:T(8,128)S(1)}, u32[]{:S(2)}, u32[]{:S(2)}) collective-permute-start(f32[112,128]{1,0:T(8,128)S(1)} %plus.4.after_ref.refs_1_), channel_id=1, source_target_pairs={{0,32},{1,33},{2,34},{3,35},{4,36},{5,37},{6,38},{7,39},{8,40},{9,... | collective-permute-start | bytes 172040 | tf_op jit(solution)/shard_map/ppermute | solution.py:414
  46.3 4.8 %collective-permute-start.11 = (f32[112,128]{1,0:T(8,128)S(1)}, f32[112,128]{1,0:T(8,128)S(1)}, u32[]{:S(2)}, u32[]{:S(2)}) collective-permute-start(f32[112,128]{1,0:T(8,128)S(1)} %plus.4.after_ref.refs_1_), channel_id=1, source_target_pairs={{0,48},{1,49},{2,50},{3,51},{4,52},{5,53},{6,54},{7,55},{8,56},{9,... | collective-permute-start | bytes 172040 | tf_op jit(solution)/shard_map/ppermute | solution.py:414
  47.0 4.2 %collective-permute-start.12 = (f32[112,128]{1,0:T(8,128)S(1)}, f32[112,128]{1,0:T(8,128)S(1)}, u32[]{:S(2)}, u32[]{:S(2)}) collective-permute-start(f32[112,128]{1,0:T(8,128)S(1)} %plus.4.after_ref.refs_1_), channel_id=1, source_target_pairs={{0,16},{1,17},{2,18},{3,19},{4,20},{5,21},{6,22},{7,23},{8,24},{9,... | collective-permute-start | bytes 172040 | tf_op jit(solution)/shard_map/ppermute | solution.py:414
  47.7 6.8 %copy-start.1 = (bf16[4,640,128]{2,1,0:T(8,128)(2,1)S(1)}, bf16[4,640,128]{2,1,0:T(8,128)(2,1)}, u32[]{:S(2)}) copy-start(bf16[4,640,128]{2,1,0:T(8,128)(2,1)} %get-tuple-element.40.planes_ref) | copy-start | bytes 1966084
  51.3 6.5 %collective-permute-start.13 = (f32[112,128]{1,0:T(8,128)S(1)}, f32[112,128]{1,0:T(8,128)S(1)}, u32[]{:S(2)}, u32[]{:S(2)}) collective-permute-start(f32[112,128]{1,0:T(8,128)S(1)} %plus.5.after_ref.refs_1_), channel_id=1, source_target_pairs={{0,128},{1,129},{2,130},{3,131},{4,132},{5,133},{6,134},{7,135},{8... | collective-permute-start | bytes 172040 | tf_op jit(solution)/shard_map/ppermute | solution.py:414
  52.9 5.0 %collective-permute-start.14 = (f32[112,128]{1,0:T(8,128)S(1)}, f32[112,128]{1,0:T(8,128)S(1)}, u32[]{:S(2)}, u32[]{:S(2)}) collective-permute-start(f32[112,128]{1,0:T(8,128)S(1)} %plus.5.after_ref.refs_1_), channel_id=1, source_target_pairs={{0,192},{1,193},{2,194},{3,195},{4,196},{5,197},{6,198},{7,199},{8... | collective-permute-start | bytes 172040 | tf_op jit(solution)/shard_map/ppermute | solution.py:414
  54.5 5.4 %collective-permute-start.15 = (f32[112,128]{1,0:T(8,128)S(1)}, f32[112,128]{1,0:T(8,128)S(1)}, u32[]{:S(2)}, u32[]{:S(2)}) collective-permute-start(f32[112,128]{1,0:T(8,128)S(1)} %plus.5.after_ref.refs_1_), channel_id=1, source_target_pairs={{0,64},{1,65},{2,66},{3,67},{4,68},{5,69},{6,70},{7,71},{8,72},{9,... | collective-permute-start | bytes 172040 | tf_op jit(solution)/shard_map/ppermute | solution.py:414
  54.5 7.6 %copy-start.2 = (bf16[4,640,128]{2,1,0:T(8,128)(2,1)S(1)}, bf16[4,640,128]{2,1,0:T(8,128)(2,1)}, u32[]{:S(2)}) copy-start(bf16[4,640,128]{2,1,0:T(8,128)(2,1)} %get-tuple-element.55.planes_ref) | copy-start | bytes 1966084
  59.9 7.0 %collective-permute-start.16 = (f32[112,128]{1,0:T(8,128)S(1)}, f32[112,128]{1,0:T(8,128)S(1)}, u32[]{:S(2)}, u32[]{:S(2)}) collective-permute-start(f32[112,128]{1,0:T(8,128)S(1)} %plus.6.after_ref.refs_1_), channel_id=1, source_target_pairs={{0,8},{1,9},{2,10},{3,11},{4,12},{5,13},{6,14},{7,15},{8,0},{9,1},... | collective-permute-start | bytes 172040 | tf_op jit(solution)/shard_map/ppermute | solution.py:414
  62.1 6.5 %copy-start = (bf16[4,640,128]{2,1,0:T(8,128)(2,1)S(1)}, bf16[4,640,128]{2,1,0:T(8,128)(2,1)}, u32[]{:S(2)}) copy-start(bf16[4,640,128]{2,1,0:T(8,128)(2,1)} %get-tuple-element.53.planes_ref) | copy-start | bytes 1966084
  66.9 5.0 %collective-permute-start.17 = (f32[112,128]{1,0:T(8,128)S(1)}, f32[112,128]{1,0:T(8,128)S(1)}, u32[]{:S(2)}, u32[]{:S(2)}) collective-permute-start(f32[112,128]{1,0:T(8,128)S(1)} %plus.7.after_ref.refs_0_), channel_id=1, source_target_pairs={{0,6},{1,7},{2,0},{3,1},{4,2},{5,3},{6,4},{7,5},{8,14},{9,15},{10,... | collective-permute-start | bytes 172040 | tf_op jit(solution)/shard_map/ppermute | solution.py:414
  67.7 4.6 %collective-permute-start.18 = (f32[112,128]{1,0:T(8,128)S(1)}, f32[112,128]{1,0:T(8,128)S(1)}, u32[]{:S(2)}, u32[]{:S(2)}) collective-permute-start(f32[112,128]{1,0:T(8,128)S(1)} %plus.7.after_ref.refs_0_), channel_id=1, source_target_pairs={{0,4},{1,5},{2,6},{3,7},{4,0},{5,1},{6,2},{7,3},{8,12},{9,13},{10,... | collective-permute-start | bytes 172040 | tf_op jit(solution)/shard_map/ppermute | solution.py:414
  67.7 5.1 %collective-permute-start.19 = (f32[112,128]{1,0:T(8,128)S(1)}, f32[112,128]{1,0:T(8,128)S(1)}, u32[]{:S(2)}, u32[]{:S(2)}) collective-permute-start(f32[112,128]{1,0:T(8,128)S(1)} %plus.7.after_ref.refs_0_), channel_id=1, source_target_pairs={{0,2},{1,3},{2,4},{3,5},{4,6},{5,7},{6,0},{7,1},{8,10},{9,11},{10,... | collective-permute-start | bytes 172040 | tf_op jit(solution)/shard_map/ppermute | solution.py:414
  72.9 8.4 %collective-permute-start.20 = (f32[448,128]{1,0:T(8,128)S(1)}, f32[448,128]{1,0:T(8,128)S(1)}, u32[]{:S(2)}, u32[]{:S(2)}) collective-permute-start(f32[448,128]{1,0:T(8,128)S(1)} %assemble.1.mine_ref), channel_id=1, source_target_pairs={{0,1},{1,0},{2,3},{3,2},{4,5},{5,4},{6,7},{7,6},{8,9},{9,8},{10,11... | collective-permute-start | bytes 688136 | tf_op jit(solution)/shard_map/ppermute | solution.py:414

commit v3 on v2

--- a/solution.py
+++ b/solution.py
@@ -414,6 +414,15 @@
     return lax.ppermute(x, AXES, shift_pairs(key, by))
 
 
+def swap_along_z(x, partner):
+    pairs = []
+    for i in range(N_DEV):
+        v = coords(i)
+        z = partner[v[2] * 4 + v[0]]
+        pairs.append((i, z % 4 * 64 + ((v[1] * 2 + z // 4) * 4 + v[3]) * 2 + v[4]))
+    return lax.ppermute(x, AXES, pairs)
+
+
 def plus(terms, token=None):
     vmem = pl.BlockSpec(memory_space=pltpu.VMEM)
     tokens = [] if token is None else [token]
@@ -533,11 +542,13 @@
     conv_out, token = conv(xa, forward, 0, part)
     part = plus([part] + got, token)
 
-    got = [send(part, "zl", s) for s in (2, 3, 1)]
+    part = plus([part, swap_along_z(part, (1, 0, 3, 2, 5, 4, 7, 6))])
+
+    got = swap_along_z(part, (7, 2, 1, 4, 3, 6, 5, 0))
     conv_out, token = conv(xb, forward, 1, part, conv_out)
-    part = plus([part] + got, token)
-
-    got = send(part, "zh", 1)
+    part = plus([part, got], token)
+
+    got = swap_along_z(part, (3, 6, 5, 0, 7, 2, 1, 4))
     grad_features, token = conv(ga, backward, 0, part)
     part = plus([part, got], token)
 

time: 82.3 us -> 80.8 us (0.982)
  waiting for transfers between devices: 9.91 us -> 8.81 us
  starting transfers between devices: 45.2 us -> 44.3 us
    ppermute x15 -> x11, starting transfers between devices: 30.3 us -> 25.4 us  [send(): return lax.ppermute(x, AXES, shift_pairs(key, by))]
    ppermute x0 -> x3, starting transfers between devices: none -> 4.03 us  [swap_along_z(): return lax.ppermute(x, AXES, pairs)]
    ppermute x15 -> x11, waiting for transfers between devices: 9.48 us -> 5.72 us  [send(): return lax.ppermute(x, AXES, shift_pairs(key, by))]
    ppermute x0 -> x3, waiting for transfers between devices: none -> 2.66 us  [swap_along_z(): return lax.ppermute(x, AXES, pairs)]
  transfers between devices with their start and end apart: 21 -> 20, of which waited for: 10 -> 10; matrix products, arithmetic and copies ran while one was open for 1% -> 1% of each run, Pallas kernels for 20% -> 21%
where the time goes in v3:
time: 80.8 us; the launch traced here: 80.5 us
  starting transfers between devices  44.3 us (55%)
  Pallas kernels  25.3 us (31%)
  waiting for transfers between devices  8.81 us (11%)
  local copies, waits for them, and re-layouts  1.11 us (1%)
  between operations  0.92 us (1%)
    ppermute x11, starting transfers between devices, send(): return lax.ppermute(x, AXES, shift_pairs(key, by))  25.4 us
    pallas_call x4, Pallas kernels, conv(): pl.pallas_call(functools.partial(conv_kernel, half), in_specs=[vmem, vmem...  13.6 us
    ppermute x11, waiting for transfers between devices, send(): return lax.ppermute(x, AXES, shift_pairs(key, by))  5.72 us
    pallas_call x1, Pallas kernels, planes_and_terms(): pl.pallas_call(terms_kernel, in_specs=[pl.BlockSpec(memory_space=pltpu.SM...  5.66 us
    ppermute x1, starting transfers between devices, shards(): below_line = lax.ppermute(high_line, 'slab', rise)  4.16 us
    ppermute x3, starting transfers between devices, swap_along_z(): return lax.ppermute(x, AXES, pairs)  4.03 us
    ppermute x1, starting transfers between devices, shards(): pair = lax.ppermute(to_pair, 'tile', [(i, i ^ 1) for i in range(64)])  3.33 us
    ppermute x1, starting transfers between devices, shards(): below = lax.ppermute(high, 'slab', rise)  2.92 us
  transfers between devices with their start and end apart: 20, of which 10 were waited for; matrix products, arithmetic and copies ran while one was open for 1% of the time, Pallas kernels for 21%

profile of v3, /device:TPU:1, one launch (start us, length us, event | category | flops | bytes accessed | tf_op | source)
XLA Modules:
  0.0 80.5 jit_solution(6936212542616419587)
XLA Ops:
  0.6 1.6 %edges.1 = (bf16[256,128]{1,0:T(8,128)(2,1)S(1)}, bf16[256,128]{1,0:T(8,128)(2,1)S(1)}, bf16[8,64,512]{2,1,0:T(8,128)(2,1)S(1)}, bf16[8,64,512]{2,1,0:T(8,128)(2,1)S(1)}) custom-call(s32[1]{0:T(128)} %bitcast.core_ref.me_ref, bf16[8,64,512]{2,1,0:T(8,128)(2,1)} %x_ref.1, bf16[8,64,512]{2,1,0:T(8,128)(2,1)} %g_ref.1), custom_call_target="tpu_custom_call" | custom-call | tf_op jit(solution)/shard_map/edges/pallas_call | solution.py:77
  2.3 3.3 %collective-permute-start.2 = (bf16[256,128]{1,0:T(8,128)(2,1)S(1)}, bf16[256,128]{1,0:T(8,128)(2,1)S(1)}, u32[]{:S(2)}, u32[]{:S(2)}) collective-permute-start(bf16[256,128]{1,0:T(8,128)(2,1)S(1)} %get-tuple-element.36), channel_id=1, source_target_pairs={{0,1},{1,0},{2,3},{3,2},{4,5},{5,4},{6,7},{7,6},{8,9},{9,8},{10,11... | collective-permute-start | bytes 196616 | tf_op jit(solution)/shard_map/ppermute | solution.py:519
  5.6 1.9 %collective-permute-start.3 = (bf16[256,128]{1,0:T(8,128)(2,1)S(1)}, bf16[256,128]{1,0:T(8,128)(2,1)S(1)}, u32[]{:S(2)}, u32[]{:S(2)}) collective-permute-start(bf16[256,128]{1,0:T(8,128)(2,1)S(1)} %get-tuple-element.37), channel_id=1, source_target_pairs={{1,2},{3,4},{5,6},{7,8},{9,10},{11,12},{13,14},{15,16},{17,18},{19... | collective-permute-start | bytes 196616 | tf_op jit(solution)/shard_map/ppermute | solution.py:518
  7.7 2.9 %collective-permute-start = (bf16[8,64,128]{2,1,0:T(8,128)(2,1)S(1)}, bf16[8,64,128]{2,1,0:T(8,128)(2,1)S(1)}, u32[]{:S(2)}, u32[]{:S(2)}) collective-permute-start(bf16[8,64,128]{2,1,0:T(8,128)(2,1)S(1)} %get-tuple-element.34), channel_id=1, source_target_pairs={{0,64},{64,128},{128,192},{1,65},{65,129},{129,193},{2,66},{66,130... | collective-permute-start | bytes 393224 | tf_op jit(solution)/shard_map/ppermute | solution.py:522
  10.6 1.3 %collective-permute-start.1 = (bf16[8,64,128]{2,1,0:T(8,128)(2,1)S(1)}, bf16[8,64,128]{2,1,0:T(8,128)(2,1)S(1)}, u32[]{:S(2)}, u32[]{:S(2)}) collective-permute-start(bf16[8,64,128]{2,1,0:T(8,128)(2,1)S(1)} %get-tuple-element.35), channel_id=1, source_target_pairs={{64,0},{128,64},{192,128},{65,1},{129,65},{193,129},{66,2},{130,66... | collective-permute-start | bytes 393224 | tf_op jit(solution)/shard_map/ppermute | solution.py:523
  12.0 4.2 %collective-permute-start.4 = (bf16[64,128]{1,0:T(8,128)(2,1)S(1)}, bf16[64,128]{1,0:T(8,128)(2,1)S(1)}, u32[]{:S(2)}, u32[]{:S(2)}) collective-permute-start(bf16[64,128]{1,0:T(8,128)(2,1)S(1)} %get-tuple-element.38), channel_id=1, source_target_pairs={{0,64},{64,128},{128,192},{1,65},{65,129},{129,193},{2,66},{66,130... | collective-permute-start | bytes 49160 | tf_op jit(solution)/shard_map/ppermute | solution.py:525
  16.2 1.3 %collective-permute-start.5 = (bf16[64,128]{1,0:T(8,128)(2,1)S(1)}, bf16[64,128]{1,0:T(8,128)(2,1)S(1)}, u32[]{:S(2)}, u32[]{:S(2)}) collective-permute-start(bf16[64,128]{1,0:T(8,128)(2,1)S(1)} %get-tuple-element.39), channel_id=1, source_target_pairs={{64,0},{128,64},{192,128},{65,1},{129,65},{193,129},{66,2},{130,66... | collective-permute-start | bytes 49160 | tf_op jit(solution)/shard_map/ppermute | solution.py:526
  17.5 0.8 pad_dynamic-slice_fusion
  18.5 1.9 %places.1.place_ref = bf16[3,768,1024]{2,1,0:T(8,128)(2,1)S(1)} custom-call(s32[1]{0:T(128)} %bitcast.core_ref.me_ref, s32[96]{0:T(128)S(1)} %reshape.16.table_ref), custom_call_target="tpu_custom_call" | custom-call | tf_op jit(solution)/shard_map/places/pallas_call | solution.py:203
  20.9 5.7 %terms.1 = (bf16[4,640,128]{2,1,0:T(8,128)(2,1)S(1)}, bf16[4,640,128]{2,1,0:T(8,128)(2,1)}, bf16[4,640,128]{2,1,0:T(8,128)(2,1)}, bf16[4,640,128]{2,1,0:T(8,128)...) custom-call(s32[1]{0:T(128)} %bitcast.core_ref.me_ref, bf16[3,768,1024]{2,1,0:T(8,128)(2,1)S(1)} %places.1.place_ref, ...), custom_call_target="tpu_custom_call" | custom-call | flops 10000000000 | bytes 10000000 | tf_op jit(solution)/shard_map/terms/pallas_call | solution.py:312
  26.7 1.4 %collective-permute-done.6.got_ref = f32[448,128]{1,0:T(8,128)S(1)} collective-permute-done((f32[448,128]{1,0:T(8,128)S(1)}, f32[448,128]{1,0:T(8,128)S(1)}, u32[]{:S(2)}, u32[]{:S(2)}) %collective-permute-start.6) | collective-permute-done | bytes 229408 | tf_op jit(solution)/shard_map/ppermute | solution.py:414
  28.1 3.6 %collective-permute-start.7 = (f32[112,128]{1,0:T(8,128)S(1)}, f32[112,128]{1,0:T(8,128)S(1)}, u32[]{:S(2)}, u32[]{:S(2)}) collective-permute-start(f32[112,128]{1,0:T(8,128)S(1)} %get-tuple-element.47), channel_id=1, source_target_pairs={{0,4},{1,5},{2,6},{3,7},{4,0},{5,1},{6,2},{7,3},{8,12},{9,13},{10,... | collective-permute-start | bytes 172040 | tf_op jit(solution)/shard_map/ppermute | solution.py:414
  31.8 3.4 %collective-permute-start.8 = (f32[112,128]{1,0:T(8,128)S(1)}, f32[112,128]{1,0:T(8,128)S(1)}, u32[]{:S(2)}, u32[]{:S(2)}) collective-permute-start(f32[112,128]{1,0:T(8,128)S(1)} %get-tuple-element.48), channel_id=1, source_target_pairs={{0,6},{1,7},{2,0},{3,1},{4,2},{5,3},{6,4},{7,5},{8,14},{9,15},{10,... | collective-permute-start | bytes 172040 | tf_op jit(solution)/shard_map/ppermute | solution.py:414
  35.8 1.3 %weights.1 = (bf16[576,192]{1,0:T(8,128)(2,1)S(1)}, bf16[576,192]{1,0:T(8,128)(2,1)S(1)}, f32[8,128]{1,0:T(8,128)S(1)}) custom-call(f32[112,128]{1,0:T(8,128)S(1)} %get-tuple-element.43.after_ref.refs_1_, s32[4,128,8]{2,1,0:T(8,128)S(1)} %copy.10.blocks_ref, bf16[64,1728]{1,0:T(8,128)(2,1)} %weight_hbm.1), custom_call_target="tpu_custom_call" | custom-call | tf_op jit(solution)/shard_map/weights/pallas_call | solution.py:151
  37.2 1.6 %collective-permute-done.8.refs_3_ = f32[112,128]{1,0:T(8,128)S(1)} collective-permute-done((f32[112,128]{1,0:T(8,128)S(1)}, f32[112,128]{1,0:T(8,128)S(1)}, u32[]{:S(2)}, u32[]{:S(2)}) %collective-permute-start.8) | collective-permute-done | bytes 57376 | tf_op jit(solution)/shard_map/ppermute | solution.py:414
  39.4 6.8 %collective-permute-start.10 = (f32[112,128]{1,0:T(8,128)S(1)}, f32[112,128]{1,0:T(8,128)S(1)}, u32[]{:S(2)}, u32[]{:S(2)}) collective-permute-start(f32[112,128]{1,0:T(8,128)S(1)} %plus.5.after_ref.refs_1_), channel_id=1, source_target_pairs={{0,32},{1,33},{2,34},{3,35},{4,36},{5,37},{6,38},{7,39},{8,40},{9,... | collective-permute-start | bytes 172040 | tf_op jit(solution)/shard_map/ppermute | solution.py:414
  46.3 0.8 collective-permute-start.11
  47.0 0.7 collective-permute-start.12
  47.7 3.4 %conv.4 = (bf16[8,64,512]{2,1,0:T(8,128)(2,1)}, f32[8,128]{1,0:T(8,128)S(1)}) custom-call(bf16[4,640,128]{2,1,0:T(8,128)(2,1)S(1)} %get-tuple-element.45.planes_ref, bf16[576,192]{1,0:T(8,128)(2,1)S(1)} %get-tuple-element.44.weight_ref, f32[112,128]{1,0:T(8,128)S(1)} %plus.5.after_ref.refs_1_), custom_call_target="tpu_custom_call" | custom-call | flops 3000000000 | bytes 1000000 | tf_op jit(solution)/shard_map/conv/pallas_call | solution.py:378
  51.3 1.1 %collective-permute-start.13 = (f32[112,128]{1,0:T(8,128)S(1)}, f32[112,128]{1,0:T(8,128)S(1)}, u32[]{:S(2)}, u32[]{:S(2)}) collective-permute-start(f32[112,128]{1,0:T(8,128)S(1)} %plus.6.refs_0_), channel_id=1, source_target_pairs={{0,64},{1,65},{2,66},{3,67},{4,68},{5,69},{6,70},{7,71},{8,72},{9,... | collective-permute-start | bytes 172040 | tf_op jit(solution)/shard_map/ppermute | solution.py:423
  52.4 2.0 %collective-permute-done.13.refs_1_ = f32[112,128]{1,0:T(8,128)S(1)} collective-permute-done((f32[112,128]{1,0:T(8,128)S(1)}, f32[112,128]{1,0:T(8,128)S(1)}, u32[]{:S(2)}, u32[]{:S(2)}) %collective-permute-start.13) | collective-permute-done | bytes 57376 | tf_op jit(solution)/shard_map/ppermute | solution.py:423
  54.4 2.1 %collective-permute-start.14 = (f32[112,128]{1,0:T(8,128)S(1)}, f32[112,128]{1,0:T(8,128)S(1)}, u32[]{:S(2)}, u32[]{:S(2)}) collective-permute-start(f32[112,128]{1,0:T(8,128)S(1)} %plus.7.after_ref.refs_1_), channel_id=1, source_target_pairs={{0,200},{1,201},{2,202},{3,203},{4,204},{5,205},{6,206},{7,207},{8... | collective-permute-start | bytes 172040 | tf_op jit(solution)/shard_map/ppermute | solution.py:423
  56.5 3.4 %conv.5 = (bf16[8,64,512]{2,1,0:T(8,128)(2,1)}, f32[8,128]{1,0:T(8,128)S(1)}) custom-call(bf16[4,640,128]{2,1,0:T(8,128)(2,1)S(1)} %copy-done.1, bf16[576,192]{1,0:T(8,128)(2,1)S(1)} %get-tuple-element.44.weight_ref, f32[112,128]{1,0:T(8,128)S(1)} %plus.7.after_ref.refs_1_, ...), custom_call_target="tpu_custom_call", output_to_operand_aliasing={{0}: (3, {})} | custom-call | flops 3000000000 | bytes 1000000 | tf_op jit(solution)/shard_map/conv/pallas_call | solution.py:378
  59.9 0.9 %collective-permute-start.15 = (f32[112,128]{1,0:T(8,128)S(1)}, f32[112,128]{1,0:T(8,128)S(1)}, u32[]{:S(2)}, u32[]{:S(2)}) collective-permute-start(f32[112,128]{1,0:T(8,128)S(1)} %plus.8.after_ref.refs_1_), channel_id=1, source_target_pairs={{0,192},{1,193},{2,194},{3,195},{4,196},{5,197},{6,198},{7,199},{8... | collective-permute-start | bytes 172040 | tf_op jit(solution)/shard_map/ppermute | solution.py:423
  60.8 3.4 %conv.6 = (bf16[8,64,512]{2,1,0:T(8,128)(2,1)}, f32[8,128]{1,0:T(8,128)S(1)}) custom-call(bf16[4,640,128]{2,1,0:T(8,128)(2,1)S(1)} %copy-done.2, bf16[576,192]{1,0:T(8,128)(2,1)S(1)} %get-tuple-element.54.weight_ref, f32[112,128]{1,0:T(8,128)S(1)} %plus.8.after_ref.refs_1_), custom_call_target="tpu_custom_call" | custom-call | flops 3000000000 | bytes 1000000 | tf_op jit(solution)/shard_map/conv/pallas_call | solution.py:378
  64.2 0.7 collective-permute-done.15.refs_2_
  64.9 2.1 %collective-permute-start.16 = (f32[112,128]{1,0:T(8,128)S(1)}, f32[112,128]{1,0:T(8,128)S(1)}, u32[]{:S(2)}, u32[]{:S(2)}) collective-permute-start(f32[112,128]{1,0:T(8,128)S(1)} %plus.9.after_ref.refs_0_), channel_id=1, source_target_pairs={{0,6},{1,7},{2,0},{3,1},{4,2},{5,3},{6,4},{7,5},{8,14},{9,15},{10,... | collective-permute-start | bytes 172040 | tf_op jit(solution)/shard_map/ppermute | solution.py:414
  66.9 0.7 collective-permute-start.18
  67.6 3.4 %conv.7 = (bf16[8,64,512]{2,1,0:T(8,128)(2,1)}, f32[8,128]{1,0:T(8,128)S(1)}) custom-call(bf16[4,640,128]{2,1,0:T(8,128)(2,1)S(1)} %copy-done, bf16[576,192]{1,0:T(8,128)(2,1)S(1)} %get-tuple-element.54.weight_ref, f32[112,128]{1,0:T(8,128)S(1)} %plus.9.after_ref.refs_0_, bf16[8,64,512]{2,1,0:T(8,128)(2,1)} %get-tuple-element.58.refs_0_), custom_call_target="tpu_custom_call", output_to_operand_aliasing={{0}: (3, {})} | custom-call | flops 3000000000 | bytes 1000000 | tf_op jit(solution)/shard_map/conv/pallas_call | solution.py:378
  71.8 6.7 %collective-permute-start.19 = (f32[448,128]{1,0:T(8,128)S(1)}, f32[448,128]{1,0:T(8,128)S(1)}, u32[]{:S(2)}, u32[]{:S(2)}) collective-permute-start(f32[448,128]{1,0:T(8,128)S(1)} %assemble.1.mine_ref), channel_id=1, source_target_pairs={{0,1},{1,0},{2,3},{3,2},{4,5},{5,4},{6,7},{7,6},{8,9},{9,8},{10,11... | collective-permute-start | bytes 688136 | tf_op jit(solution)/shard_map/ppermute | solution.py:414
  78.5 1.1 %collective-permute-done.19.other_ref = f32[448,128]{1,0:T(8,128)S(1)} collective-permute-done((f32[448,128]{1,0:T(8,128)S(1)}, f32[448,128]{1,0:T(8,128)S(1)}, u32[]{:S(2)}, u32[]{:S(2)}) %collective-permute-start.19) | collective-permute-done | bytes 229408 | tf_op jit(solution)/shard_map/ppermute | solution.py:414
  79.7 0.8 finish.1
  (38 shorter events, 3.2 us)
Async XLA Ops:
  2.3 9.6 %collective-permute-start.2 = (bf16[256,128]{1,0:T(8,128)(2,1)S(1)}, bf16[256,128]{1,0:T(8,128)(2,1)S(1)}, u32[]{:S(2)}, u32[]{:S(2)}) collective-permute-start(bf16[256,128]{1,0:T(8,128)(2,1)S(1)} %get-tuple-element.36), channel_id=1, source_target_pairs={{0,1},{1,0},{2,3},{3,2},{4,5},{5,4},{6,7},{7,6},{8,9},{9,8},{10,11... | collective-permute-start | bytes 196616 | tf_op jit(solution)/shard_map/ppermute | solution.py:519
  5.6 6.3 %collective-permute-start.3 = (bf16[256,128]{1,0:T(8,128)(2,1)S(1)}, bf16[256,128]{1,0:T(8,128)(2,1)S(1)}, u32[]{:S(2)}, u32[]{:S(2)}) collective-permute-start(bf16[256,128]{1,0:T(8,128)(2,1)S(1)} %get-tuple-element.37), channel_id=1, source_target_pairs={{1,2},{3,4},{5,6},{7,8},{9,10},{11,12},{13,14},{15,16},{17,18},{19... | collective-permute-start | bytes 196616 | tf_op jit(solution)/shard_map/ppermute | solution.py:518
  7.7 13.2 %collective-permute-start = (bf16[8,64,128]{2,1,0:T(8,128)(2,1)S(1)}, bf16[8,64,128]{2,1,0:T(8,128)(2,1)S(1)}, u32[]{:S(2)}, u32[]{:S(2)}) collective-permute-start(bf16[8,64,128]{2,1,0:T(8,128)(2,1)S(1)} %get-tuple-element.34), channel_id=1, source_target_pairs={{0,64},{64,128},{128,192},{1,65},{65,129},{129,193},{2,66},{66,130... | collective-permute-start | bytes 393224 | tf_op jit(solution)/shard_map/ppermute | solution.py:522
  10.6 10.2 %collective-permute-start.1 = (bf16[8,64,128]{2,1,0:T(8,128)(2,1)S(1)}, bf16[8,64,128]{2,1,0:T(8,128)(2,1)S(1)}, u32[]{:S(2)}, u32[]{:S(2)}) collective-permute-start(bf16[8,64,128]{2,1,0:T(8,128)(2,1)S(1)} %get-tuple-element.35), channel_id=1, source_target_pairs={{64,0},{128,64},{192,128},{65,1},{129,65},{193,129},{66,2},{130,66... | collective-permute-start | bytes 393224 | tf_op jit(solution)/shard_map/ppermute | solution.py:523
  12.0 8.4 %collective-permute-start.4 = (bf16[64,128]{1,0:T(8,128)(2,1)S(1)}, bf16[64,128]{1,0:T(8,128)(2,1)S(1)}, u32[]{:S(2)}, u32[]{:S(2)}) collective-permute-start(bf16[64,128]{1,0:T(8,128)(2,1)S(1)} %get-tuple-element.38), channel_id=1, source_target_pairs={{0,64},{64,128},{128,192},{1,65},{65,129},{129,193},{2,66},{66,130... | collective-permute-start | bytes 49160 | tf_op jit(solution)/shard_map/ppermute | solution.py:525
  16.2 4.7 %collective-permute-start.5 = (bf16[64,128]{1,0:T(8,128)(2,1)S(1)}, bf16[64,128]{1,0:T(8,128)(2,1)S(1)}, u32[]{:S(2)}, u32[]{:S(2)}) collective-permute-start(bf16[64,128]{1,0:T(8,128)(2,1)S(1)} %get-tuple-element.39), channel_id=1, source_target_pairs={{64,0},{128,64},{192,128},{65,1},{129,65},{193,129},{66,2},{130,66... | collective-permute-start | bytes 49160 | tf_op jit(solution)/shard_map/ppermute | solution.py:526
  20.4 15.3 %copy-start.3 = (s32[4,128,8]{1,2,0:T(8,128)S(1)}, s32[4,128,8]{1,2,0:T(8,128)}, u32[]{:S(2)}) copy-start(s32[4,128,8]{1,2,0:T(8,128)} %param.7) | copy-start | bytes 49156
  26.5 1.6 %collective-permute-start.6 = (f32[448,128]{1,0:T(8,128)S(1)}, f32[448,128]{1,0:T(8,128)S(1)}, u32[]{:S(2)}, u32[]{:S(2)}) collective-permute-start(f32[448,128]{1,0:T(8,128)S(1)} %get-tuple-element.42), channel_id=1, source_target_pairs={{0,1},{1,0},{2,3},{3,2},{4,5},{5,4},{6,7},{7,6},{8,9},{9,8},{10,11... | collective-permute-start | bytes 688136 | tf_op jit(solution)/shard_map/ppermute | solution.py:414
  28.1 9.0 %collective-permute-start.7 = (f32[112,128]{1,0:T(8,128)S(1)}, f32[112,128]{1,0:T(8,128)S(1)}, u32[]{:S(2)}, u32[]{:S(2)}) collective-permute-start(f32[112,128]{1,0:T(8,128)S(1)} %get-tuple-element.47), channel_id=1, source_target_pairs={{0,4},{1,5},{2,6},{3,7},{4,0},{5,1},{6,2},{7,3},{8,12},{9,13},{10,... | collective-permute-start | bytes 172040 | tf_op jit(solution)/shard_map/ppermute | solution.py:414
  31.8 7.1 %collective-permute-start.8 = (f32[112,128]{1,0:T(8,128)S(1)}, f32[112,128]{1,0:T(8,128)S(1)}, u32[]{:S(2)}, u32[]{:S(2)}) collective-permute-start(f32[112,128]{1,0:T(8,128)S(1)} %get-tuple-element.48), channel_id=1, source_target_pairs={{0,6},{1,7},{2,0},{3,1},{4,2},{5,3},{6,4},{7,5},{8,14},{9,15},{10,... | collective-permute-start | bytes 172040 | tf_op jit(solution)/shard_map/ppermute | solution.py:414
  35.2 4.2 %collective-permute-start.9 = (f32[112,128]{1,0:T(8,128)S(1)}, f32[112,128]{1,0:T(8,128)S(1)}, u32[]{:S(2)}, u32[]{:S(2)}) collective-permute-start(f32[112,128]{1,0:T(8,128)S(1)} %get-tuple-element.49), channel_id=1, source_target_pairs={{0,2},{1,3},{2,4},{3,5},{4,6},{5,7},{6,0},{7,1},{8,10},{9,11},{10,... | collective-permute-start | bytes 172040 | tf_op jit(solution)/shard_map/ppermute | solution.py:414
  39.4 11.7 %collective-permute-start.10 = (f32[112,128]{1,0:T(8,128)S(1)}, f32[112,128]{1,0:T(8,128)S(1)}, u32[]{:S(2)}, u32[]{:S(2)}) collective-permute-start(f32[112,128]{1,0:T(8,128)S(1)} %plus.5.after_ref.refs_1_), channel_id=1, source_target_pairs={{0,32},{1,33},{2,34},{3,35},{4,36},{5,37},{6,38},{7,39},{8,40},{9,... | collective-permute-start | bytes 172040 | tf_op jit(solution)/shard_map/ppermute | solution.py:414
  46.3 4.9 %collective-permute-start.11 = (f32[112,128]{1,0:T(8,128)S(1)}, f32[112,128]{1,0:T(8,128)S(1)}, u32[]{:S(2)}, u32[]{:S(2)}) collective-permute-start(f32[112,128]{1,0:T(8,128)S(1)} %plus.5.after_ref.refs_1_), channel_id=1, source_target_pairs={{0,48},{1,49},{2,50},{3,51},{4,52},{5,53},{6,54},{7,55},{8,56},{9,... | collective-permute-start | bytes 172040 | tf_op jit(solution)/shard_map/ppermute | solution.py:414
  47.0 4.2 %collective-permute-start.12 = (f32[112,128]{1,0:T(8,128)S(1)}, f32[112,128]{1,0:T(8,128)S(1)}, u32[]{:S(2)}, u32[]{:S(2)}) collective-permute-start(f32[112,128]{1,0:T(8,128)S(1)} %plus.5.after_ref.refs_1_), channel_id=1, source_target_pairs={{0,16},{1,17},{2,18},{3,19},{4,20},{5,21},{6,22},{7,23},{8,24},{9,... | collective-permute-start | bytes 172040 | tf_op jit(solution)/shard_map/ppermute | solution.py:414
  47.7 8.8 %copy-start.1 = (bf16[4,640,128]{2,1,0:T(8,128)(2,1)S(1)}, bf16[4,640,128]{2,1,0:T(8,128)(2,1)}, u32[]{:S(2)}) copy-start(bf16[4,640,128]{2,1,0:T(8,128)(2,1)} %get-tuple-element.40.planes_ref) | copy-start | bytes 1966084
  51.3 3.1 %collective-permute-start.13 = (f32[112,128]{1,0:T(8,128)S(1)}, f32[112,128]{1,0:T(8,128)S(1)}, u32[]{:S(2)}, u32[]{:S(2)}) collective-permute-start(f32[112,128]{1,0:T(8,128)S(1)} %plus.6.refs_0_), channel_id=1, source_target_pairs={{0,64},{1,65},{2,66},{3,67},{4,68},{5,69},{6,70},{7,71},{8,72},{9,... | collective-permute-start | bytes 172040 | tf_op jit(solution)/shard_map/ppermute | solution.py:423
  54.4 5.5 %collective-permute-start.14 = (f32[112,128]{1,0:T(8,128)S(1)}, f32[112,128]{1,0:T(8,128)S(1)}, u32[]{:S(2)}, u32[]{:S(2)}) collective-permute-start(f32[112,128]{1,0:T(8,128)S(1)} %plus.7.after_ref.refs_1_), channel_id=1, source_target_pairs={{0,200},{1,201},{2,202},{3,203},{4,204},{5,205},{6,206},{7,207},{8... | collective-permute-start | bytes 172040 | tf_op jit(solution)/shard_map/ppermute | solution.py:423
  56.5 4.3 %copy-start.2 = (bf16[4,640,128]{2,1,0:T(8,128)(2,1)S(1)}, bf16[4,640,128]{2,1,0:T(8,128)(2,1)}, u32[]{:S(2)}) copy-start(bf16[4,640,128]{2,1,0:T(8,128)(2,1)} %get-tuple-element.55.planes_ref) | copy-start | bytes 1966084
  59.9 4.9 %collective-permute-start.15 = (f32[112,128]{1,0:T(8,128)S(1)}, f32[112,128]{1,0:T(8,128)S(1)}, u32[]{:S(2)}, u32[]{:S(2)}) collective-permute-start(f32[112,128]{1,0:T(8,128)S(1)} %plus.8.after_ref.refs_1_), channel_id=1, source_target_pairs={{0,192},{1,193},{2,194},{3,195},{4,196},{5,197},{6,198},{7,199},{8... | collective-permute-start | bytes 172040 | tf_op jit(solution)/shard_map/ppermute | solution.py:423
  60.8 6.8 %copy-start = (bf16[4,640,128]{2,1,0:T(8,128)(2,1)S(1)}, bf16[4,640,128]{2,1,0:T(8,128)(2,1)}, u32[]{:S(2)}) copy-start(bf16[4,640,128]{2,1,0:T(8,128)(2,1)} %get-tuple-element.53.planes_ref) | copy-start | bytes 1966084
  64.9 6.2 %collective-permute-start.16 = (f32[112,128]{1,0:T(8,128)S(1)}, f32[112,128]{1,0:T(8,128)S(1)}, u32[]{:S(2)}, u32[]{:S(2)}) collective-permute-start(f32[112,128]{1,0:T(8,128)S(1)} %plus.9.after_ref.refs_0_), channel_id=1, source_target_pairs={{0,6},{1,7},{2,0},{3,1},{4,2},{5,3},{6,4},{7,5},{8,14},{9,15},{10,... | collective-permute-start | bytes 172040 | tf_op jit(solution)/shard_map/ppermute | solution.py:414
  66.9 4.6 %collective-permute-start.17 = (f32[112,128]{1,0:T(8,128)S(1)}, f32[112,128]{1,0:T(8,128)S(1)}, u32[]{:S(2)}, u32[]{:S(2)}) collective-permute-start(f32[112,128]{1,0:T(8,128)S(1)} %plus.9.after_ref.refs_0_), channel_id=1, source_target_pairs={{0,4},{1,5},{2,6},{3,7},{4,0},{5,1},{6,2},{7,3},{8,12},{9,13},{10,... | collective-permute-start | bytes 172040 | tf_op jit(solution)/shard_map/ppermute | solution.py:414
  66.9 4.9 %collective-permute-start.18 = (f32[112,128]{1,0:T(8,128)S(1)}, f32[112,128]{1,0:T(8,128)S(1)}, u32[]{:S(2)}, u32[]{:S(2)}) collective-permute-start(f32[112,128]{1,0:T(8,128)S(1)} %plus.9.after_ref.refs_0_), channel_id=1, source_target_pairs={{0,2},{1,3},{2,4},{3,5},{4,6},{5,7},{6,0},{7,1},{8,10},{9,11},{10,... | collective-permute-start | bytes 172040 | tf_op jit(solution)/shard_map/ppermute | solution.py:414
  71.8 7.8 %collective-permute-start.19 = (f32[448,128]{1,0:T(8,128)S(1)}, f32[448,128]{1,0:T(8,128)S(1)}, u32[]{:S(2)}, u32[]{:S(2)}) collective-permute-start(f32[448,128]{1,0:T(8,128)S(1)} %assemble.1.mine_ref), channel_id=1, source_target_pairs={{0,1},{1,0},{2,3},{3,2},{4,5},{5,4},{6,7},{7,6},{8,9},{9,8},{10,11... | collective-permute-start | bytes 688136 | tf_op jit(solution)/shard_map/ppermute | solution.py:414
